TPU v7x, 32 devices: a whole 2x2x4 slice. The times are simulated.
32 devices in a mesh: seq: 4 (over x, core), branch: 2 (over y), tensor: 4 (over z).
Axes of the slice: x: 2, y: 2, z: 4, core: 2. Of those that a mesh axis runs over, the one named last changes fastest.
Arguments:
- tokens: bfloat16 [1024, 2048], P('seq', ('branch', 'tensor')), may hold values from -6 to 6
- cotangent: bfloat16 [1024, 2048], P('seq', ('branch', 'tensor')), may hold values from -6 to 6
- documents: int32 [1024], P('seq'), may hold values from 0 to 2, as said below
- positions: int32 [1024], P('seq'), may hold values from 0 to 1023, as said below
- project_weight: bfloat16 [2048, 6144], P(None, 'tensor'), may hold values from -0.125 to 0.125
- offsets: float32 [6144], P('tensor'), may hold values from -0.75 to 0.75
- output_weight: bfloat16 [2048, 2048], P(None, 'tensor'), may hold values from -0.75 to 0.75
- up_weight: bfloat16 [2048, 8192], P(None, 'tensor'), may hold values from -0.125 to 0.125
- hidden_bias: float32 [8192], P('tensor'), may hold values from -6 to 6
- down_weight: bfloat16 [2048, 8192], P(None, 'tensor'), may hold values from -0.0625 to 0.0625
- norm_gain: float32 [2, 2048], P('branch'), may hold values from 0.1 to 1.9
- norm_bias: float32 [2, 2048], P('branch'), may hold values from -4 to 4
- residual_bias: float32 [2, 2048], P('branch'), may hold values from -4 to 4
Outputs:
- layer_out: bfloat16 [1024, 2048], P('seq', ('branch', 'tensor'))
- input_grad: float32 [1024, 2048], P('seq', ('branch', 'tensor'))
- project_grad: float32 [2048, 6144], P(('seq', 'branch'), 'tensor')
- output_grad: float32 [2048, 2048], P(('seq', 'branch'), 'tensor')
- up_grad: float32 [2048, 8192], P(('seq', 'branch'), 'tensor')
- down_grad: float32 [2048, 8192], P(('seq', 'branch'), 'tensor')
- offsets_grad: float32 [6144], replicated
- hidden_grad: float32 [8192], replicated
- gain_grad: float32 [2, 2048], replicated
- center_grad: float32 [2, 2048], replicated
- residual_grad: float32 [2, 2048], replicated
Inputs may be any that keep to these rules, and one draw needn't show every extreme that they name: `documents`: document numbers never fall along the tokens; each document is one contiguous run of tokens and none is empty; document 1 begins within the first 256 tokens and ends within the last 256. Within a document positions start at 0 and rise by 1 from each token to the next.
All inputs are finite; a program needn't handle non-finite values.
Results may differ from a plain program's by a relative error of at most 0.015.
Values may be sent and summed in bfloat16 or wider, within the bound.
A program may use at most 192 MiB of HBM per device.

v0:
```python
from functools import partial

import jax
import jax.numpy as jnp
from jax import lax
from jax.experimental import pallas as pl
from jax.experimental.pallas import tpu as pltpu
from jax.sharding import PartitionSpec as P

HEAD_DIM = 128
ROT = 32


norm_eps = 1e-05
rope_base = 10000.0
masked_score = -1e30


def passed_along(value, axis, steps):
    count = lax.axis_size(axis)
    pairs = [(source, (source + steps) % count) for source in range(count)]
    return lax.ppermute(value, axis, pairs)


def shifted(array, axis, by):
    count = lax.axis_size(axis)
    pairs = [(i, i + by) for i in range(count) if 0 <= i + by < count]
    return lax.ppermute(array, axis, pairs)


def layer_norm(values, gain_row, shift_row):
    average = jnp.mean(values, axis=-1, keepdims=True)
    centered = values - average
    variance = jnp.mean(centered * centered, axis=-1, keepdims=True)
    return centered * lax.rsqrt(variance + norm_eps) * gain_row + shift_row


def rope_tables(places):
    half_rot = ROT // 2
    frequency = rope_base ** (-(2.0 * jnp.arange(half_rot, dtype=jnp.float32)) / ROT)
    angles = places.astype(jnp.float32)[:, None] * frequency[None, :]
    return (jnp.cos(angles), jnp.sin(angles))


def rotate(values, cosine, sine_rows, direction):
    half_rot = ROT // 2
    first_half = values[..., :half_rot]
    second_half = values[..., half_rot:ROT]
    cos_table = cosine[:, None, :]
    sin_table = direction * sine_rows[:, None, :]
    return jnp.concatenate(
        [
            first_half * cos_table - second_half * sin_table,
            second_half * cos_table + first_half * sin_table,
            values[..., ROT:],
        ],
        axis=-1,
    )


def contract_rows(first_side, second_side):
    return lax.dot_general(
        first_side, second_side, (((0,), (0,)), ((), ())), preferred_element_type=jnp.float32
    )


def contract_cols(first_side, second_side):
    return lax.dot_general(
        first_side, second_side, (((1,), (1,)), ((), ())), preferred_element_type=jnp.float32
    )


def on_device(
    tokens,
    cotangent,
    documents,
    positions,
    project_weight,
    offsets,
    output_weight,
    up_weight,
    hidden_bias,
    down_weight,
    norm_gain,
    norm_bias,
    residual_bias,
):
    tok_rows = tokens.shape[0]
    model_width = up_weight.shape[0]
    attn_width = output_weight.shape[1]
    local_heads = attn_width // HEAD_DIM
    hidden_local = up_weight.shape[1]
    seq_count = lax.axis_size("seq")
    seq_index = lax.axis_index("seq")
    branch_index = lax.axis_index("branch")
    tensor_index = lax.axis_index("tensor")
    is_attention = branch_index == 0
    lead_tensor = tensor_index == 0
    score_scale = HEAD_DIM ** (-0.5)
    local_index = jnp.arange(tok_rows, dtype=jnp.int32)
    query_index = seq_index * tok_rows + local_index
    full_tokens, full_cotangent = (
        lax.all_gather(tokens, ("branch", "tensor"), axis=1, tiled=True),
        lax.all_gather(cotangent, ("branch", "tensor"), axis=1, tiled=True),
    )
    gain_row = norm_gain[0]
    shift_row = norm_bias[0]
    normed, norm_pullback = jax.vjp(
        layer_norm, full_tokens.astype(jnp.float32), gain_row, shift_row
    )
    normed_low = normed.astype(jnp.bfloat16)
    cosine, sine_rows = rope_tables(positions)
    zeros_heads = jnp.zeros((tok_rows, attn_width), jnp.bfloat16)
    zeros_hidden = jnp.zeros((tok_rows, hidden_local), jnp.float32)
    hidden_zero = jnp.zeros((tok_rows, hidden_local), jnp.bfloat16)
    zeros_stats = jnp.zeros((local_heads, tok_rows), jnp.float32)
    grad_zero = jnp.zeros((tok_rows, local_heads, HEAD_DIM), jnp.float32)

    def attention_front(unused):
        packed = jnp.dot(normed_low, project_weight, preferred_element_type=jnp.float32) + offsets
        packed = packed.reshape(tok_rows, local_heads, 3, HEAD_DIM)
        query_rot = rotate(packed[:, :, 0], cosine, sine_rows, 1.0).reshape(tok_rows, attn_width)
        key_rot = rotate(packed[:, :, 1], cosine, sine_rows, 1.0).reshape(tok_rows, attn_width)
        value_rows = packed[:, :, 2].reshape(tok_rows, attn_width)
        return (
            query_rot.astype(jnp.bfloat16),
            key_rot.astype(jnp.bfloat16),
            value_rows.astype(jnp.bfloat16),
            zeros_hidden,
            hidden_zero,
        )

    def feed_front(unused):
        up_rows = jnp.dot(normed_low, up_weight, preferred_element_type=jnp.float32) + hidden_bias
        active = jax.nn.gelu(up_rows, approximate=False).astype(jnp.bfloat16)
        return (zeros_heads, zeros_heads, zeros_heads, up_rows, active)

    query_low, key_low, value_low, up_rows, active = lax.cond(
        is_attention, attention_front, feed_front, 0
    )
    query_heads = query_low.reshape(tok_rows, local_heads, HEAD_DIM)

    def absorb(totals, key_rows, value_rows, key_ids, offset):
        key_count = key_rows.shape[0]
        key_index = offset + jnp.arange(key_count, dtype=jnp.int32)
        visible = (documents[:, None] == key_ids[None, :]) & (
            key_index[None, :] <= query_index[:, None]
        )

        def update(running):
            run_max, run_sum, run_acc = running
            scores = (
                jnp.einsum(
                    "qhd,khd->hqk",
                    query_heads,
                    key_rows.reshape(key_count, local_heads, HEAD_DIM),
                    preferred_element_type=jnp.float32,
                )
                * score_scale
            )
            masked = jnp.where(visible[None], scores, masked_score)
            new_max = jnp.maximum(run_max, jnp.max(masked, axis=-1))
            weights = jnp.where(visible[None], jnp.exp(masked - new_max[:, :, None]), 0.0)
            factor = jnp.exp(run_max - new_max)
            blended = jnp.einsum(
                "hqk,khd->qhd",
                weights.astype(jnp.bfloat16),
                value_rows.reshape(key_count, local_heads, HEAD_DIM),
                preferred_element_type=jnp.float32,
            )
            return (
                new_max,
                run_sum * factor + jnp.sum(weights, axis=-1),
                run_acc * factor.T[:, :, None] + blended,
            )

        def unchanged(running):
            return running

        return lax.cond(is_attention & jnp.any(visible), update, unchanged, totals)

    initial = (jnp.full((local_heads, tok_rows), masked_score, jnp.float32), zeros_stats, grad_zero)
    totals = initial
    key_rows = lax.all_gather(key_low, "seq", axis=0, tiled=True)
    value_rows = lax.all_gather(value_low, "seq", axis=0, tiled=True)
    key_ids = lax.all_gather(documents, "seq", axis=0, tiled=True)
    key_count = key_rows.shape[0]
    groups = key_count // tok_rows

    def absorb_group(running, sliced):
        return (absorb(running, sliced[0], sliced[1], sliced[2], sliced[3]), None)

    starts = tok_rows * jnp.arange(groups, dtype=jnp.int32)
    stacked = (
        key_rows.reshape(groups, tok_rows, attn_width),
        value_rows.reshape(groups, tok_rows, attn_width),
        key_ids.reshape(groups, tok_rows),
        starts,
    )
    totals, unused = lax.scan(absorb_group, totals, stacked)
    run_max, run_sum, run_acc = totals

    def attention_out(unused):
        attended = run_acc / run_sum.T[:, :, None]
        attended_low = attended.reshape(tok_rows, attn_width).astype(jnp.bfloat16)
        return (
            contract_cols(attended_low, output_weight),
            attended,
            attended_low,
            run_max + jnp.log(run_sum),
        )

    def feed_out(unused):
        return (contract_cols(active, down_weight), grad_zero, zeros_heads, zeros_stats)

    branch_out, attended, attended_low, lse_rows = lax.cond(
        is_attention, attention_out, feed_out, 0
    )
    branch_out = branch_out + jnp.where(lead_tensor, residual_bias[0], 0.0)
    summed = lax.psum_scatter(
        branch_out.astype(jnp.bfloat16), ("branch", "tensor"), scatter_dimension=1, tiled=True
    ).astype(jnp.float32)
    layer_out = (tokens.astype(jnp.float32) + summed).astype(jnp.bfloat16)

    def attention_prep(unused):
        grad_low = jnp.dot(
            full_cotangent, output_weight, preferred_element_type=jnp.float32
        ).astype(jnp.bfloat16)
        delta_rows = jnp.sum(
            grad_low.reshape(tok_rows, local_heads, HEAD_DIM).astype(jnp.float32) * attended,
            axis=-1,
        ).T
        return (grad_low, delta_rows, hidden_zero)

    def feed_prep(unused):
        active_grad = jnp.dot(full_cotangent, down_weight, preferred_element_type=jnp.float32)
        gelu_value, gelu_pullback = jax.vjp(partial(jax.nn.gelu, approximate=False), up_rows)
        return (zeros_heads, zeros_stats, gelu_pullback(active_grad)[0].astype(jnp.bfloat16))

    grad_low, delta_rows, hidden_low = lax.cond(is_attention, attention_prep, feed_prep, 0)

    def block_grads(
        query_rows,
        grad_rows,
        query_lse,
        query_delta,
        query_ids,
        query_place,
        key_rows,
        value_rows,
        key_ids,
        key_place,
    ):
        visible = (query_ids[:, None] == key_ids[None, :]) & (
            key_place[None, :] <= query_place[:, None]
        )

        def compute(unused):
            query_part_heads = query_rows.reshape(tok_rows, local_heads, HEAD_DIM)
            grad_heads = grad_rows.reshape(tok_rows, local_heads, HEAD_DIM)
            key_heads = key_rows.reshape(tok_rows, local_heads, HEAD_DIM)
            value_heads = value_rows.reshape(tok_rows, local_heads, HEAD_DIM)
            scores = (
                jnp.einsum(
                    "qhd,khd->hqk", query_part_heads, key_heads, preferred_element_type=jnp.float32
                )
                * score_scale
            )
            weights = jnp.exp(
                jnp.where(visible[None], scores - query_lse[:, :, None], masked_score)
            )
            value_part = jnp.einsum(
                "hqk,qhd->khd",
                weights.astype(jnp.bfloat16),
                grad_heads,
                preferred_element_type=jnp.float32,
            )
            weight_grad = jnp.einsum(
                "qhd,khd->hqk", grad_heads, value_heads, preferred_element_type=jnp.float32
            )
            score_grad = (weights * (weight_grad - query_delta[:, :, None])).astype(jnp.bfloat16)
            query_part = (
                jnp.einsum(
                    "hqk,khd->qhd", score_grad, key_heads, preferred_element_type=jnp.float32
                )
                * score_scale
            )
            key_part = (
                jnp.einsum(
                    "hqk,qhd->khd", score_grad, query_part_heads, preferred_element_type=jnp.float32
                )
                * score_scale
            )
            return (query_part, key_part, value_part)

        def nothing(unused):
            return (grad_zero, grad_zero, grad_zero)

        return lax.cond(is_attention & jnp.any(visible), compute, nothing, 0)

    def send_grads(key_acc, value_acc):
        return (
            passed_along(key_acc.astype(jnp.bfloat16), "seq", 1).astype(key_acc.dtype),
            passed_along(value_acc.astype(jnp.bfloat16), "seq", 1).astype(value_acc.dtype),
        )

    def key_step(cycle_state, unused):
        key_rows, value_rows, key_ids, key_acc, value_acc, hop_count, query_acc = cycle_state
        source = (seq_index - hop_count) % seq_count
        partial_terms = block_grads(
            query_low,
            grad_low,
            lse_rows,
            delta_rows,
            documents,
            query_index,
            key_rows,
            value_rows,
            key_ids,
            source * tok_rows + local_index,
        )
        key_rows, value_rows, key_ids = shifted((key_rows, value_rows, key_ids), "seq", 1)
        key_acc, value_acc = send_grads(key_acc + partial_terms[1], value_acc + partial_terms[2])
        return (
            (
                key_rows,
                value_rows,
                key_ids,
                key_acc,
                value_acc,
                hop_count + 1,
                query_acc + partial_terms[0],
            ),
            None,
        )

    start_state = (key_low, value_low, documents, grad_zero, grad_zero, jnp.int32(0), grad_zero)
    cycle_state, unused = lax.scan(key_step, start_state, None, length=seq_count - 1)
    key_rows, value_rows, key_ids, key_acc, value_acc, hop_count, query_acc = cycle_state
    source = (seq_index - hop_count) % seq_count
    partial_terms = block_grads(
        query_low,
        grad_low,
        lse_rows,
        delta_rows,
        documents,
        query_index,
        key_rows,
        value_rows,
        key_ids,
        source * tok_rows + local_index,
    )
    key_grad, value_grad = send_grads(key_acc + partial_terms[1], value_acc + partial_terms[2])
    query_grad = query_acc + partial_terms[0]

    def attention_tail(unused):
        query_back = rotate(query_grad, cosine, sine_rows, -1.0)
        key_back = rotate(key_grad, cosine, sine_rows, -1.0)
        packed_grad = (
            jnp.stack([query_back, key_back, value_grad], axis=2)
            .reshape(tok_rows, 3 * attn_width)
            .astype(jnp.bfloat16)
        )
        return (contract_cols(packed_grad, project_weight), packed_grad)

    def feed_tail(unused):
        return (
            contract_cols(hidden_low, up_weight),
            jnp.zeros((tok_rows, 3 * attn_width), jnp.bfloat16),
        )

    norm_grad, packed_grad = lax.cond(is_attention, attention_tail, feed_tail, 0)
    input_part, gain_part, shift_part = norm_pullback(norm_grad)
    input_grad = lax.psum_scatter(
        input_part.astype(jnp.bfloat16), ("branch", "tensor"), scatter_dimension=1, tiled=True
    ).astype(jnp.float32) + cotangent.astype(jnp.float32)

    def attention_rows(unused):
        return jnp.concatenate(
            [
                contract_rows(normed_low, packed_grad),
                contract_rows(full_cotangent, attended_low),
                jnp.zeros(
                    (
                        model_width
                        // (seq_count * lax.axis_size("branch"))
                        * lax.axis_size(("seq", "branch")),
                        2 * hidden_local,
                    ),
                    jnp.float32,
                ),
            ],
            axis=1,
        )

    def feed_rows(unused):
        return jnp.concatenate(
            [
                jnp.zeros(
                    (
                        model_width
                        // (seq_count * lax.axis_size("branch"))
                        * lax.axis_size(("seq", "branch")),
                        4 * attn_width,
                    ),
                    jnp.float32,
                ),
                contract_rows(normed_low, hidden_low),
                contract_rows(full_cotangent, active),
            ],
            axis=1,
        )

    shares = lax.psum_scatter(
        lax.cond(is_attention, attention_rows, feed_rows, 0).astype(jnp.bfloat16),
        ("seq", "branch"),
        scatter_dimension=0,
        tiled=True,
    ).astype(jnp.float32)
    project_grad = shares[:, : 3 * attn_width]
    output_grad = shares[:, 3 * attn_width : 4 * attn_width]
    up_grad = shares[:, 4 * attn_width : 4 * attn_width + hidden_local]
    down_grad = shares[:, 4 * attn_width + hidden_local :]
    offsets_part = lax.dynamic_update_slice(
        jnp.zeros((3 * model_width,), jnp.float32),
        jnp.sum(packed_grad, axis=0, dtype=jnp.float32),
        (tensor_index * (3 * attn_width),),
    )
    hidden_part = lax.dynamic_update_slice(
        jnp.zeros((hidden_local * lax.axis_size("tensor"),), jnp.float32),
        jnp.sum(hidden_low, axis=0, dtype=jnp.float32),
        (tensor_index * hidden_local,),
    )
    pair_zero = jnp.zeros((2, model_width), jnp.float32)
    gain_rows = lax.dynamic_update_slice(
        pair_zero, gain_part[None, :], (branch_index, jnp.int32(0))
    )
    shift_rows = lax.dynamic_update_slice(
        pair_zero, shift_part[None, :], (branch_index, jnp.int32(0))
    )
    column_sums = jnp.where(lead_tensor, jnp.sum(full_cotangent, axis=0, dtype=jnp.float32), 0.0)
    residual_rows = lax.dynamic_update_slice(
        pair_zero, column_sums[None, :], (branch_index, jnp.int32(0))
    )
    offsets_grad, hidden_grad, gain_grad, center_grad, residual_grad = lax.psum(
        (offsets_part, hidden_part, gain_rows, shift_rows, residual_rows),
        ("seq", "branch", "tensor"),
    )
    return (
        layer_out,
        input_grad,
        project_grad,
        output_grad,
        up_grad,
        down_grad,
        offsets_grad,
        hidden_grad,
        gain_grad,
        center_grad,
        residual_grad,
    )


MESH = pl.DeviceIdType.MESH
bf16, f32 = jnp.bfloat16, jnp.float32


def place():
    s, b, t = lax.axis_index("seq"), lax.axis_index("branch"), lax.axis_index("tensor")
    return s, b, t, s // 2, s % 2


def flip(value, bit):
    return value + bit - 2 * bit * value


def flip4(value, k):
    return 2 * flip(value // 2, k // 2) + flip(value % 2, k % 2)


def plane_peer(k):
    s, b, t, x, c = place()
    return (2 * flip(x, k // 2) + c, flip(b, k % 2), t)


def grid_peer(k):
    s, b, t, x, c = place()
    return (s, flip(b, k // 4), flip4(t, k % 4))


def sibling():
    s, b, t, x, c = place()
    return (flip4(s, 1), b, t)


def meet(devices):
    barrier = pltpu.get_barrier_semaphore()
    for device in devices:
        pl.semaphore_signal(barrier, inc=1, device_id=device, device_id_type=MESH)
    pl.semaphore_wait(barrier, len(devices))


def at(index, size):
    return pl.ds(pl.multiple_of(index * size, size), size)


def dot(first, second):
    return jnp.dot(first, second, preferred_element_type=f32)


def turned(values, tables, direction):
    lane = lax.broadcasted_iota(jnp.int32, values.shape, 1)
    swapped = jnp.where(
        lane < ROT // 2,
        pltpu.roll(values, HEAD_DIM - ROT // 2, 1),
        pltpu.roll(values, ROT // 2, 1),
    )
    sines = jnp.where(lane < ROT, tables[:, HEAD_DIM:], 0.0)
    return values * tables[:, :HEAD_DIM] + (direction * sines) * swapped


def layer_kernel(
    tok, cot, table, rows, offs, hbias, wp_h, wo_h, wu_h, wd_h,
    layer_o, grad_o, project_o, output_o, up_o, down_o, sums_o,
    wp, wo, wu, wd, xg, cg, tables, rows2, xh, inv, n0, n1, xb, gd, act, hid, hs, heads, att, pack,
    attf, lse, dk_acc, dv_acc, ob, ro, gb, rg, acco, accg, xs, cs, n0t, n1t, ct, own, other, recv,
    usum, pair, near, sems, local,
):
    s, b, t, x, c = place()
    m, j = 2 * x + b, 4 * b + t
    slot = 4 * x + 2 * c + b
    scale = HEAD_DIM ** -0.5
    mine = at(m, 128)
    used = {"sem": 0, "local": 0}
    sent = []

    def send(src, dst, device):
        index = used["sem"]
        used["sem"] += 1
        copy = pltpu.make_async_remote_copy(
            src_ref=src, dst_ref=dst, send_sem=sems.at[0, index], recv_sem=sems.at[1, index],
            device_id=device, device_id_type=MESH)
        copy.start()
        sent.append(copy)
        return copy

    def move(src, dst):
        index = used["local"]
        used["local"] += 1
        copy = pltpu.make_async_copy(src, dst, local.at[index])
        copy.start()
        return copy

    def arrive(copies):
        for copy in copies:
            copy.wait_recv()

    def direct(view):
        return [send(view(m), view(m), plane_peer(k)) for k in (2, 1)]

    def relay(copies, half):
        out = []
        for i, k in enumerate((2, 1)):
            copies[i].wait_recv()
            part = half(flip4(m, k), i)
            out.append(send(part, part, plane_peer(3 - k)))
        return out

    def loop(count, body):
        def step(i, carry):
            body(i)
            return carry
        lax.fori_loop(0, count, step, 0)

    usum[...] = jnp.zeros_like(usum)
    wp_load, wu_load = move(wp_h, wp), move(wu_h, wu)
    wo_load, wd_load = move(wo_h, wo), move(wd_h, wd)
    meet([grid_peer(k) for k in range(1, 8)] + [plane_peer(2), plane_peer(3)]
         + [(flip4(s, k), b, t) for k in (1, 3)])

    def gather(src, dst):
        copies = []
        for k in (1, 2, 3, 4, 5, 6, 7):
            peer = grid_peer(k)
            copies.append(send(src.at[at(peer[1], 128)], dst.at[:, at(j, 256)], peer))
        return copies, move(src.at[at(b, 128)], dst.at[:, at(j, 256)])

    x_copies, x_own = gather(tok, xg)
    row_copy = send(rows, rows2.at[b], grid_peer(4))
    row_own = move(rows, rows2.at[b])
    table_copies = [send(table, tables.at[at(s, 256)], (flip4(s, k), b, t)) for k in (1, 2, 3)]
    table_own = move(table, tables.at[at(s, 256)])
    arrive(x_copies)
    x_own.wait()
    g_copies, g_own = gather(cot, cg)
    arrive([row_copy])
    row_own.wait()

    def norm(i):
        part = at(i, 16)
        v = xg[part, :].astype(f32)
        centered = v - jnp.mean(v, axis=-1, keepdims=True)
        inverse = lax.rsqrt(jnp.mean(centered * centered, axis=-1, keepdims=True) + norm_eps)
        hat = centered * inverse
        xh[part, :] = hat
        xb[part, :] = hat.astype(bf16)
        inv[part, :] = jnp.broadcast_to(inverse, (16, 128))
        n0[part, :] = (hat * rows2[0, 0:1, :] + rows2[0, 1:2, :]).astype(bf16)
        n1[part, :] = (hat * rows2[1, 0:1, :] + rows2[1, 1:2, :]).astype(bf16)

    loop(8, norm)

    def slices(src, dst):
        copies, kept = [], []
        for half in (0, 1):
            cols = pl.ds(half * 256, 256)
            for k in (1, 2, 3):
                there = flip4(m, k)
                block = 4 * (there // 2) + 2 * half + there % 2
                copies.append(send(src.at[:, at(block, 256)], dst.at[mine, cols], plane_peer(k)))
            kept.append(move(src.at[:, at(4 * x + 2 * half + b, 256)], dst.at[mine, cols]))
        return copies, kept

    wp_load.wait()

    def project(h):
        p = dot(n0[...], wp[:, at(h, 384)]) + offs[:, at(h, 384)]
        tab = table[at(b, 128), :]
        hs[h, :, 0:128] = turned(p[:, 0:128], tab, 1.0).astype(bf16)
        hs[h, :, 128:256] = turned(p[:, 128:256], tab, 1.0).astype(bf16)
        hs[h, :, 256:384] = p[:, 256:384].astype(bf16)

    loop(4, project)

    def to_heads(cols):
        copies = [send(hs.at[flip4(m, k), :, cols], heads.at[at(slot, 128), cols], plane_peer(k))
                  for k in (3, 2, 1)]
        return copies, move(hs.at[m, :, cols], heads.at[at(slot, 128), cols])

    def to_sibling(copies, kept, cols):
        arrive(copies)
        kept.wait()
        parts = [heads.at[pl.ds(512 * i + 256 * c, 256), cols] for i in (0, 1)]
        arrive([send(part, part, sibling()) for part in parts])

    qkv_cols, up_cols = pl.ds(0, 384), pl.ds(384, 128)
    qkv_copies, qkv_own = to_heads(qkv_cols)
    xs_copies, xs_own = slices(xb, xs)
    wu_load.wait()

    def feed(n):
        cols = at(n, 256)
        u = dot(n1[...], wu[:, cols]) + hbias[:, cols]
        phi = 0.5 + 0.5 * lax.erf(u * 0.7071067811865476)
        act[mine, cols] = (u * phi).astype(bf16)
        gd[:, cols] = phi + u * (0.3989422804014327 * jnp.exp(-0.5 * u * u))

    loop(8, feed)
    act_view = lambda i: act.at[at(i, 128)]
    act_half = lambda i, h: act.at[pl.ds(pl.multiple_of(128 * i + 64 * h, 64), 64)]
    hid_view = lambda i: hid.at[at(i, 128)]
    hid_half = lambda i, h: hid.at[pl.ds(pl.multiple_of(128 * i + 64 * h, 64), 64)]
    att_view = lambda i: att.at[:, at(i, 128)]
    att_half = lambda i, h: att.at[pl.ds(256 * h, 256), at(i, 128)]
    pack_view = lambda i: pack.at[:, at(i, 384)]
    pack_half = lambda i, h: pack.at[pl.ds(256 * h, 256), at(i, 384)]
    act_copies = direct(act_view)

    to_sibling(qkv_copies, qkv_own, qkv_cols)
    arrive(table_copies)
    table_own.wait()

    def score_rows(i):
        part = at(i, 256)
        scores = contract_cols(heads[part, 0:128], heads[:, 128:256]) * scale
        start = tables[part, 128:256][:, 127:128]
        query = (i * 256 + lax.broadcasted_iota(jnp.int32, (256, 1), 0)).astype(f32)
        key = lax.broadcasted_iota(jnp.int32, (256, 1024), 1).astype(f32)
        return scores, (key <= query) & (key >= start)

    def forward(i):
        part = at(i, 256)
        scores, visible = score_rows(i)
        masked = jnp.where(visible, scores, masked_score)
        top = jnp.max(masked, axis=-1, keepdims=True)
        weights = jnp.where(visible, jnp.exp(masked - top), 0.0)
        total = jnp.sum(weights, axis=-1, keepdims=True)
        attf[part, :] = dot(weights.astype(bf16), heads[:, 256:384]) / total
        lse[part, :] = jnp.broadcast_to(top + jnp.log(total), (256, 128))

    loop(4, forward)
    for i in (0, 1):
        att[pl.ds(256 * i, 256), at(m, 128)] = attf[pl.ds(512 * i + 256 * c, 256), :].astype(bf16)
    att_copies = direct(att_view)

    arrive(g_copies)
    g_own.wait()
    wo_load.wait()

    def head_grads(n):
        p = dot(cg[...], wo[:, at(n, 256)]).astype(bf16)
        hs[2 * n, :, 384:512] = p[:, :128]
        hs[2 * n + 1, :, 384:512] = p[:, 128:]

    loop(2, head_grads)
    up_copies, up_own = to_heads(up_cols)
    cs_copies, cs_own = slices(cg, cs)
    wd_load.wait()

    def hidden(n):
        cols = at(n, 256)
        low = (dot(cg[...], wd[:, cols]) * gd[:, cols]).astype(bf16)
        hid[mine, cols] = low
        usum[6:7, cols] = jnp.sum(low.astype(f32), axis=0, keepdims=True)
        usum[4:5, cols] = jnp.sum(cg[:, cols].astype(f32), axis=0, keepdims=True)

    loop(8, hidden)

    to_sibling(up_copies, up_own, up_cols)
    dk_acc[...] = jnp.zeros_like(dk_acc)
    dv_acc[...] = jnp.zeros_like(dv_acc)

    def backward(i):
        part = at(i, 256)
        scores, visible = score_rows(i)
        probs = jnp.where(visible, jnp.exp(jnp.where(visible, scores, masked_score) - lse[part, 0:1]), 0.0)
        up = heads[part, 384:512]
        delta = jnp.sum(up.astype(f32) * attf[part, :], axis=-1, keepdims=True)
        grads = (probs * (contract_cols(up, heads[:, 256:384]) - delta)).astype(bf16)
        dv_acc[...] += contract_rows(probs.astype(bf16), up)
        dk_acc[...] += contract_rows(grads, heads[part, 0:128])

        @pl.when(i % 2 == c)
        def _():
            back = dot(grads, heads[:, 128:256]) * scale
            pack[at(i // 2, 256), at(3 * m, 128)] = turned(back, tables[part, :], -1.0).astype(bf16)

    loop(4, backward)
    for i in (0, 1):
        part = pl.ds(512 * i + 256 * c, 256)
        key_back = turned(dk_acc[part, :] * scale, tables[part, :], -1.0)
        pack[pl.ds(256 * i, 256), at(3 * m + 1, 128)] = key_back.astype(bf16)
        pack[pl.ds(256 * i, 256), at(3 * m + 2, 128)] = dv_acc[part, :].astype(bf16)
    pack_copies = direct(pack_view)
    att_relays = relay(att_copies, att_half)
    act_relays = relay(act_copies, act_half)
    hid_copies = direct(hid_view)

    def feed_out(n):
        acco[n] = contract_cols(act[mine, :], wd[at(n, 256), :])

    loop(8, feed_out)

    def norm_grad(n, values, weight, which):
        cols = at(n, 256)
        ng = contract_cols(values, weight[cols, :])
        usum[which : which + 1, cols] = jnp.sum(ng * xh[:, cols], axis=0, keepdims=True)
        usum[which + 2 : which + 3, cols] = jnp.sum(ng, axis=0, keepdims=True)
        return ng * rows2[which, 0:1, cols]

    def feed_grad(n):
        accg[n] = norm_grad(n, hid[mine, :], wu, 1)

    loop(8, feed_grad)
    arrive(att_relays)

    def finish_out(n):
        ob[n] = (acco[n] + contract_cols(att[mine, :], wo[at(n, 256), :])).astype(bf16)

    loop(8, finish_out)

    def scatter(src, dst):
        copies = [send(src.at[4 * grid_peer(k)[1] + grid_peer(k)[2]], dst.at[j], grid_peer(k))
                  for k in range(1, 8)]
        return copies, move(src.at[j], dst.at[j])

    out_copies, out_own = scatter(ob, ro)
    arrive(xs_copies + cs_copies)
    for copy in xs_own + cs_own:
        copy.wait()

    def transpose_slices(i):
        part = at(i, 128)
        for half in (0, 1):
            cols = pl.ds(256 * half, 256)
            block = at(4 * x + 2 * half + b, 256)
            hat = xs[part, cols].astype(f32)
            for which, dst in ((0, n0t), (1, n1t)):
                low = hat * rows2[which, 0:1, block] + rows2[which, 1:2, block]
                dst[cols, part] = low.T.astype(bf16)
            ct[cols, part] = cs[part, cols].astype(f32).T.astype(bf16)

    loop(4, transpose_slices)

    pack_relays = relay(pack_copies, pack_half)
    arrive(pack_relays)

    def attention_grad(n):
        accg[n] += norm_grad(n, pack[mine, :], wp, 0)

    loop(8, attention_grad)
    usum[5:6, 0:1536] = jnp.sum(pack[mine, :].astype(f32), axis=0, keepdims=True)
    pair_copy = send(usum, pair, sibling())

    zero = jnp.zeros((128, 1), f32)

    def means(n, carry):
        g = accg[n]
        return (carry[0] + jnp.sum(g, axis=-1, keepdims=True),
                carry[1] + jnp.sum(g * xh[:, at(n, 256)], axis=-1, keepdims=True))

    mean, slope = lax.fori_loop(0, 8, means, (zero, zero))
    mean, slope = mean * (1.0 / 2048), slope * (1.0 / 2048)

    def finish_grad(n):
        gb[n] = (inv[:, 0:1] * (accg[n] - mean - xh[:, at(n, 256)] * slope)).astype(bf16)

    loop(8, finish_grad)
    grad_copies, grad_own = scatter(gb, rg)

    writes = []

    def matrix(lhs, rhs, count, out, base):
        for copy in writes[-1:]:
            for part in copy:
                part.wait()
        first = used["sem"]
        used["sem"] += count

        def swap(i):
            return pltpu.make_async_remote_copy(
                src_ref=other.at[base + i], dst_ref=recv.at[base + i],
                send_sem=sems.at[0, first + i], recv_sem=sems.at[1, first + i],
                device_id=sibling(), device_id_type=MESH)

        def produce(i):
            right = rhs[:, at(i, 512)]
            other[base + i] = dot(lhs[at(1 - c, 256), :], right).astype(bf16)
            swap(i).start()
            own[i] = dot(lhs[at(c, 256), :], right)

        loop(count, produce)
        done = []
        for i in range(count):
            swap(i).wait_recv()
            own[i] += recv[base + i].astype(f32)
            done.append(move(own.at[i], out.at[:, pl.ds(512 * i, 512)]))
            sent.append(swap(i))
        writes.append(done)

    arrive(act_relays)
    matrix(ct, act, 4, down_o, 0)
    hid_relays = relay(hid_copies, hid_half)
    matrix(ct, att, 1, output_o, 4)
    arrive([pair_copy])
    pair[...] += usum[...]
    near_copies = [send(pair, near.at[k - 1], plane_peer(k)) for k in (1, 2, 3)]
    matrix(n0t, pack, 3, project_o, 5)
    arrive(near_copies)
    sums_o[t] = pair[...] + near[0] + near[1] + near[2]
    sum_copies = [send(sums_o.at[t], sums_o.at[t], grid_peer(k)) for k in (1, 2, 3)]
    arrive(out_copies)
    out_own.wait()
    columns = at(j, 256)
    bias = rows2[0, 2:3, columns] + rows2[1, 2:3, columns]
    for h in (0, 1):
        part = pl.ds(128 * h, 128)
        total = bias + tok[part, :].astype(f32)
        for i in range(4):
            total = total + ro[4 * h + i].astype(f32)
        layer_o[part, :] = total.astype(bf16)
    arrive(grad_copies)
    grad_own.wait()
    for h in (0, 1):
        part = pl.ds(128 * h, 128)
        total = cot[part, :].astype(f32)
        for i in range(4):
            total = total + rg[4 * h + i].astype(f32)
        grad_o[part, :] = total
    arrive(hid_relays)
    matrix(n1t, hid, 4, up_o, 8)
    arrive(sum_copies)
    for part in writes[-1]:
        part.wait()
    for copy in sent:
        copy.wait_send()
    assert used["sem"] <= 100 and used["local"] <= 40, used


def fast_device(tokens, cotangent, documents, positions, project_weight, offsets, output_weight,
                up_weight, hidden_bias, down_weight, norm_gain, norm_bias, residual_bias):
    s = lax.axis_index("seq")
    cosine, sines = rope_tables(positions)
    token_index = s * 256 + jnp.arange(256, dtype=jnp.int32)
    start = (token_index - positions).astype(f32)
    table = jnp.concatenate([
        cosine, cosine, jnp.ones((256, HEAD_DIM - ROT), f32),
        -sines, sines, jnp.broadcast_to(start[:, None], (256, HEAD_DIM - ROT))], axis=1)
    rows = jnp.concatenate([norm_gain, norm_bias, residual_bias, jnp.zeros((5, 2048), f32)], axis=0)
    vmem, anywhere = pl.BlockSpec(memory_space=pltpu.VMEM), pl.BlockSpec(memory_space=pl.ANY)
    shape = jax.ShapeDtypeStruct
    low = lambda *size: pltpu.VMEM(size, bf16)
    full = lambda *size: pltpu.VMEM(size, f32)
    layer_out, input_grad, project_grad, output_grad, up_grad, down_grad, sums = pl.pallas_call(
        layer_kernel,
        out_shape=[
            shape((256, 256), bf16), shape((256, 256), f32), shape((256, 1536), f32),
            shape((256, 512), f32), shape((256, 2048), f32), shape((256, 2048), f32),
            shape((4, 8, 2048), f32)],
        in_specs=[vmem] * 6 + [anywhere] * 4,
        out_specs=[vmem] * 2 + [anywhere] * 4 + [vmem],
        scratch_shapes=[
            low(2048, 1536), low(2048, 512), low(2048, 2048), low(2048, 2048),
            low(128, 2048), low(128, 2048), full(1024, 256), full(2, 8, 2048),
            full(128, 2048), full(128, 128), low(128, 2048), low(128, 2048), low(128, 2048),
            full(128, 2048), low(512, 2048), low(512, 2048), low(4, 128, 512), low(1024, 512),
            low(512, 512), low(512, 1536), full(1024, 128), full(1024, 128), full(1024, 128),
            full(1024, 128), low(8, 128, 256), low(8, 128, 256), low(8, 128, 256),
            low(8, 128, 256), full(8, 128, 256), full(8, 128, 256), low(512, 512), low(512, 512),
            low(512, 512), low(512, 512), low(512, 512), full(4, 256, 512), low(12, 256, 512),
            low(12, 256, 512), full(8, 2048), full(8, 2048), full(3, 8, 2048),
            pltpu.SemaphoreType.DMA((2, 100)), pltpu.SemaphoreType.DMA((40,))],
        compiler_params=pltpu.CompilerParams(
            collective_id=0, has_side_effects=True, vmem_limit_bytes=LIMIT),
    )(tokens, cotangent, table, rows, offsets[None], hidden_bias[None], project_weight,
      output_weight, up_weight, down_weight)
    across = jnp.sum(sums[:, :4], axis=0)
    return (
        layer_out, input_grad, project_grad, output_grad, up_grad, down_grad,
        sums[:, 5, :1536].reshape(6144), sums[:, 6].reshape(8192),
        across[:2], across[2:], jnp.broadcast_to(sums[0, 4], (2, 2048)))


LIMIT = 62 << 20


def solution(mesh):
    fits = (mesh.shape["seq"], mesh.shape["branch"], mesh.shape["tensor"]) == (4, 2, 4)
    return jax.shard_map(
        fast_device if fits else on_device,
        mesh=mesh,
        in_specs=(
            P("seq", ("branch", "tensor")),
            P("seq", ("branch", "tensor")),
            P("seq"),
            P("seq"),
            P(None, "tensor"),
            P("tensor"),
            P(None, "tensor"),
            P(None, "tensor"),
            P("tensor"),
            P(None, "tensor"),
            P("branch", None),
            P("branch", None),
            P("branch", None),
        ),
        out_specs=(
            P("seq", ("branch", "tensor")),
            P("seq", ("branch", "tensor")),
            P(("seq", "branch"), "tensor"),
            P(("seq", "branch"), "tensor"),
            P(("seq", "branch"), "tensor"),
            P(("seq", "branch"), "tensor"),
            P(),
            P(),
            P(),
            P(),
            P(),
        ),
        check_vma=False,
    )
```

profile of v0, /device:TPU:0, one launch (start us, length us, event | category | flops | bytes accessed | tf_op | source)
XLA Modules:
  0.0 156.2 jit_solution(2814560920229907714)
XLA Ops:
  0.7 0.1 pad.3.clone
  0.7 0.8 subtract_convert_fusion
  1.5 1.3 broadcast_in_dim.26.offs
  2.8 1.4 maximum_maximum_fusion.rows
  4.2 0.1 broadcast_in_dim.24
  4.3 0.5 multiply_sine_fusion
  4.9 0.9 concatenate.6.table
  5.8 133.6 %shard_map.203 = (bf16[256,256]{1,0:T(8,128)(2,1)}, f32[256,256]{1,0:T(8,128)}, f32[256,1536]{1,0:T(8,128)}, f32[256,512]{1,0:T(8,128)}, f32[256,2048]{1,0:T(8,1...) custom-call(bf16[256,256]{1,0:T(8,128)(2,1)} %tok.1, bf16[256,256]{1,0:T(8,128)(2,1)} %cot.1, ...), custom_call_target="tpu_custom_call" | custom-call | tf_op jit(solution)/shard_map/pallas_call | solution.py:904
  139.4 0.8 slice.23
  140.2 0.6 broadcast_in_dim.28
  140.8 1.6 slice.18
  142.4 0.0 copy-start.2
  142.4 1.0 slice_reduce_fusion
  143.4 1.6 %slice.19 = f32[4,1,2048]{2,1,0:T(1,128)} slice(f32[4,8,2048]{2,1,0:T(8,128)} %get-tuple-element.24), slice={[0:4], [6:7], [0:2048]} | slice | bytes 65536 | tf_op jit(solution)/shard_map/slice | solution.py:930
  145.0 0.6 fusion.1
  145.7 1.6 %copy.30 = bf16[256,256]{1,0:T(8,128)(2,1)} copy(bf16[256,256]{1,0:T(8,128)(2,1)} %get-tuple-element.43) | data formatting | bytes 262144
  147.2 1.7 %copy.31 = f32[256,256]{1,0:T(8,128)} copy(f32[256,256]{1,0:T(8,128)} %get-tuple-element.44) | data formatting | bytes 524288
  148.9 0.0 copy-start.1
  148.9 2.8 %copy.32 = f32[256,1536]{1,0:T(8,128)} copy(f32[256,1536]{1,0:T(8,128)} %get-tuple-element.45) | data formatting | bytes 3145728
  151.7 0.0 copy-done.2
  151.7 0.8 copy.33
  152.5 0.0 copy-done.1
  152.5 0.0 copy-start
  152.5 1.3 copy.34
  153.8 1.0 copy-done
  154.9 1.3 copy.35
  (3 shorter events, 0.0 us)
Async XLA Ops:
  142.4 9.3 %copy-start.2 = (f32[256,512]{1,0:T(8,128)S(1)}, f32[256,512]{1,0:T(8,128)}, u32[]{:S(2)}) copy-start(f32[256,512]{1,0:T(8,128)} %get-tuple-element.46) | copy-start | bytes 1572868
  148.9 3.6 %copy-start.1 = (f32[256,2048]{1,0:T(8,128)S(1)}, f32[256,2048]{1,0:T(8,128)}, u32[]{:S(2)}) copy-start(f32[256,2048]{1,0:T(8,128)} %get-tuple-element.47) | copy-start | bytes 6291460
  152.5 2.3 %copy-start = (f32[256,2048]{1,0:T(8,128)S(1)}, f32[256,2048]{1,0:T(8,128)}, u32[]{:S(2)}) copy-start(f32[256,2048]{1,0:T(8,128)} %get-tuple-element.48) | copy-start | bytes 6291460
where the time goes:
time: 157 us; the launch traced here: 156 us
  Pallas kernels  134 us (85%)
  local copies, waits for them, and re-layouts  18.1 us (12%)
  other arithmetic  3.78 us (2%)
    pallas_call x1, Pallas kernels, fast_device(): pl.pallas_call(layer_kernel, out_shape=[shape((256, 256), bf16), shape((2...  134 us
    unnamed x12, local copies, waits for them, and re-layouts  10.5 us

commit v1 on v0

--- a/solution.py
+++ b/solution.py
@@ -508,23 +508,22 @@
     return jnp.dot(first, second, preferred_element_type=f32)
 
 
-def turned(values, tables, direction):
+def turned(values, cosine, sines):
     lane = lax.broadcasted_iota(jnp.int32, values.shape, 1)
     swapped = jnp.where(
         lane < ROT // 2,
         pltpu.roll(values, HEAD_DIM - ROT // 2, 1),
         pltpu.roll(values, ROT // 2, 1),
     )
-    sines = jnp.where(lane < ROT, tables[:, HEAD_DIM:], 0.0)
-    return values * tables[:, :HEAD_DIM] + (direction * sines) * swapped
+    return values * cosine + sines * swapped
 
 
 def layer_kernel(
-    tok, cot, table, rows, offs, hbias, wp_h, wo_h, wu_h, wd_h,
+    tok, cot, places, waves, gain, shift, residual, offs, hbias, wp_h, wo_h, wu_h, wd_h,
     layer_o, grad_o, project_o, output_o, up_o, down_o, sums_o,
-    wp, wo, wu, wd, xg, cg, tables, rows2, xh, inv, n0, n1, xb, gd, act, hid, hs, heads, att, pack,
-    attf, lse, dk_acc, dv_acc, ob, ro, gb, rg, acco, accg, xs, cs, n0t, n1t, ct, own, other, recv,
-    usum, pair, near, sems, local,
+    wp, wo, wu, wd, xg, cg, posr, starts, cosr, sinr, rows2, xh, mean_s, inv_s, n0, n1, gd, act, hid,
+    hs, heads, att, pack, attf, lse, dk_acc, dv_acc, ob, ro, gb, rg, swap_b, back_b, acco, accg,
+    n0t, n1t, ct, own, low_own, other, recv, usum, pair, near, sems, local,
 ):
     s, b, t, x, c = place()
     m, j = 2 * x + b, 4 * b + t
@@ -572,62 +571,91 @@
             return carry
         lax.fori_loop(0, count, step, 0)
 
+    def block(k):
+        return at(4 * flip(b, k // 4) + flip4(t, k % 4), 256)
+
     usum[...] = jnp.zeros_like(usum)
-    wp_load, wu_load = move(wp_h, wp), move(wu_h, wu)
-    wo_load, wd_load = move(wo_h, wo), move(wd_h, wd)
-    meet([grid_peer(k) for k in range(1, 8)] + [plane_peer(2), plane_peer(3)]
+    wp_load, wo_load = move(wp_h, wp), move(wo_h, wo)
+    wu_load, wd_load = move(wu_h, wu), move(wd_h, wd)
+    rows2[b] = jnp.zeros((8, 2048), f32)
+    rows2[b, 0:1, :] = gain[...]
+    rows2[b, 1:2, :] = shift[...]
+    rows2[b, 2:3, :] = residual[...]
+    posr[s] = jnp.broadcast_to(places[...].astype(f32), (8, 256))
+    meet([grid_peer(k) for k in (1, 2, 3, 4)] + [plane_peer(2), plane_peer(3)]
          + [(flip4(s, k), b, t) for k in (1, 3)])
 
-    def gather(src, dst):
-        copies = []
-        for k in (1, 2, 3, 4, 5, 6, 7):
-            peer = grid_peer(k)
-            copies.append(send(src.at[at(peer[1], 128)], dst.at[:, at(j, 256)], peer))
-        return copies, move(src.at[at(b, 128)], dst.at[:, at(j, 256)])
-
-    x_copies, x_own = gather(tok, xg)
-    row_copy = send(rows, rows2.at[b], grid_peer(4))
-    row_own = move(rows, rows2.at[b])
-    table_copies = [send(table, tables.at[at(s, 256)], (flip4(s, k), b, t)) for k in (1, 2, 3)]
-    table_own = move(table, tables.at[at(s, 256)])
-    arrive(x_copies)
+    def gather_first(src, dst):
+        over = send(src.at[at(1 - b, 128)], dst.at[at(flip4(m, 1), 128), at(j, 256)], grid_peer(4))
+        half = src.at[at(b, 128)]
+        copies = [send(half, dst.at[mine, at(j, 256)], grid_peer(k)) for k in (1, 3, 2)]
+        return over, copies, move(half, dst.at[mine, at(j, 256)])
+
+    def gather_second(over, dst):
+        over.wait_recv()
+        part = dst.at[mine, block(4)]
+        return [send(part, part, grid_peer(k)) for k in (1, 3, 2)]
+
+    x_over, x_near, x_own = gather_first(tok, xg)
+    row_copy = send(rows2.at[b], rows2.at[b], grid_peer(4))
+    place_copies = [send(posr.at[s], posr.at[s], (flip4(s, k), b, t)) for k in (1, 2, 3)]
+    spread = {}
+
+    def on_plane(k):
+        part = xg.at[mine, block(k)]
+        spread[k] = [send(part, part, plane_peer(i)) for i in (2, 1)]
+
     x_own.wait()
-    g_copies, g_own = gather(cot, cg)
+    on_plane(0)
+    x_far = gather_second(x_over, xg)
+    on_plane(4)
+    arrive(place_copies)
+    for i in range(4):
+        row = jnp.broadcast_to(posr[i, 0:1, :], (128, 256))
+        index = (256 * i + lax.broadcasted_iota(jnp.int32, (256, 128), 0)).astype(f32)
+        starts[pl.ds(256 * i, 256), :] = index - row.T
+    for i in (0, 1):
+        angle = posr[2 * i + c, 0:1, :] * waves[...]
+        part = pl.ds(256 * i, 256)
+        sign = jnp.where(lax.broadcasted_iota(jnp.int32, (ROT, 256), 0) < ROT // 2, -1.0, 1.0)
+        rest = jnp.zeros((HEAD_DIM - ROT, 256), f32)
+        cosr[part, :] = jnp.concatenate([jnp.cos(angle), rest + 1.0], axis=0).T
+        sinr[part, :] = jnp.concatenate([jnp.sin(angle) * sign, rest], axis=0).T
+    for i, k in enumerate((1, 3, 2)):
+        x_near[i].wait_recv()
+        on_plane(k)
+        x_far[i].wait_recv()
+        on_plane(k + 4)
+    g_over, g_near, g_own = gather_first(cot, cg)
     arrive([row_copy])
-    row_own.wait()
-
-    def norm(i):
-        part = at(i, 16)
-        v = xg[part, :].astype(f32)
-        centered = v - jnp.mean(v, axis=-1, keepdims=True)
-        inverse = lax.rsqrt(jnp.mean(centered * centered, axis=-1, keepdims=True) + norm_eps)
-        hat = centered * inverse
-        xh[part, :] = hat
-        xb[part, :] = hat.astype(bf16)
-        inv[part, :] = jnp.broadcast_to(inverse, (16, 128))
-        n0[part, :] = (hat * rows2[0, 0:1, :] + rows2[0, 1:2, :]).astype(bf16)
-        n1[part, :] = (hat * rows2[1, 0:1, :] + rows2[1, 1:2, :]).astype(bf16)
-
-    loop(8, norm)
-
-    def slices(src, dst):
-        copies, kept = [], []
-        for half in (0, 1):
-            cols = pl.ds(half * 256, 256)
-            for k in (1, 2, 3):
-                there = flip4(m, k)
-                block = 4 * (there // 2) + 2 * half + there % 2
-                copies.append(send(src.at[:, at(block, 256)], dst.at[mine, cols], plane_peer(k)))
-            kept.append(move(src.at[:, at(4 * x + 2 * half + b, 256)], dst.at[mine, cols]))
-        return copies, kept
-
+
+    def norm(which, whole):
+        def rows(i):
+            part = pl.ds(pl.multiple_of(which * 128 + 16 * i, 16), 16)
+            v = xg[part, :].astype(f32)
+            mean = jnp.mean(v, axis=-1, keepdims=True)
+            centered = v - mean
+            inverse = lax.rsqrt(jnp.mean(centered * centered, axis=-1, keepdims=True) + norm_eps)
+            hat = centered * inverse
+            mean_s[part, :] = jnp.broadcast_to(mean, (16, 128))
+            inv_s[part, :] = jnp.broadcast_to(inverse, (16, 128))
+            n1_part = pl.ds(pl.multiple_of((which % 2) * 128 + 16 * i, 16), 16)
+            n1[n1_part, :] = (hat * rows2[1, 0:1, :] + rows2[1, 1:2, :]).astype(bf16)
+            if whole:
+                xh[at(i, 16), :] = hat
+                n0[at(i, 16), :] = (hat * rows2[0, 0:1, :] + rows2[0, 1:2, :]).astype(bf16)
+
+        loop(8, rows)
+
+    norm(m, True)
+    g_far = gather_second(g_over, cg)
     wp_load.wait()
+    turn = pl.ds(pl.multiple_of(256 * x + 128 * b, 128), 128)
 
     def project(h):
         p = dot(n0[...], wp[:, at(h, 384)]) + offs[:, at(h, 384)]
-        tab = table[at(b, 128), :]
-        hs[h, :, 0:128] = turned(p[:, 0:128], tab, 1.0).astype(bf16)
-        hs[h, :, 128:256] = turned(p[:, 128:256], tab, 1.0).astype(bf16)
+        hs[h, :, 0:128] = turned(p[:, 0:128], cosr[turn, :], sinr[turn, :]).astype(bf16)
+        hs[h, :, 128:256] = turned(p[:, 128:256], cosr[turn, :], sinr[turn, :]).astype(bf16)
         hs[h, :, 256:384] = p[:, 256:384].astype(bf16)
 
     loop(4, project)
@@ -641,42 +669,64 @@
         arrive(copies)
         kept.wait()
         parts = [heads.at[pl.ds(512 * i + 256 * c, 256), cols] for i in (0, 1)]
-        arrive([send(part, part, sibling()) for part in parts])
+        return [send(part, part, sibling()) for part in parts]
 
     qkv_cols, up_cols = pl.ds(0, 384), pl.ds(384, 128)
     qkv_copies, qkv_own = to_heads(qkv_cols)
-    xs_copies, xs_own = slices(xb, xs)
+    x_relays, x_rest = [], []
+    for k in range(4):
+        spread[k][0].wait_recv()
+        part = xg.at[at(flip4(m, 2), 128), block(k)]
+        x_relays.append(send(part, part, plane_peer(1)))
+        spread[k + 4][1].wait_recv()
+        part = xg.at[at(flip4(m, 1), 128), block(k)]
+        x_relays.append(send(part, part, plane_peer(2)))
+        x_rest.append(spread[k + 4][0])
+    arrive([spread[k][1] for k in range(4)])
+    norm(flip4(m, 1), False)
     wu_load.wait()
 
-    def feed(n):
-        cols = at(n, 256)
-        u = dot(n1[...], wu[:, cols]) + hbias[:, cols]
-        phi = 0.5 + 0.5 * lax.erf(u * 0.7071067811865476)
-        act[mine, cols] = (u * phi).astype(bf16)
-        gd[:, cols] = phi + u * (0.3989422804014327 * jnp.exp(-0.5 * u * u))
-
-    loop(8, feed)
-    act_view = lambda i: act.at[at(i, 128)]
-    act_half = lambda i, h: act.at[pl.ds(pl.multiple_of(128 * i + 64 * h, 64), 64)]
-    hid_view = lambda i: hid.at[at(i, 128)]
-    hid_half = lambda i, h: hid.at[pl.ds(pl.multiple_of(128 * i + 64 * h, 64), 64)]
+    def feed(pair_index):
+        rows = at(pair_index, 256)
+
+        def tile(n):
+            cols = at(n, 256)
+            u = dot(n1[...], wu[:, cols]) + hbias[:, cols]
+            phi = 0.5 + 0.5 * lax.erf(u * 0.7071067811865476)
+            act[rows, cols] = (u * phi).astype(bf16)
+            gd[rows, cols] = (phi + u * (0.3989422804014327 * jnp.exp(-0.5 * u * u))).astype(gd.dtype)
+
+        loop(8, tile)
+
+    feed(x)
+    qkv_pair = to_sibling(qkv_copies, qkv_own, qkv_cols)
+    cg_view = lambda i: cg.at[at(i, 128)]
+    cg_half = lambda i, h: cg.at[pl.ds(pl.multiple_of(128 * i + 64 * h, 64), 64)]
     att_view = lambda i: att.at[:, at(i, 128)]
     att_half = lambda i, h: att.at[pl.ds(256 * h, 256), at(i, 128)]
     pack_view = lambda i: pack.at[:, at(i, 384)]
     pack_half = lambda i, h: pack.at[pl.ds(256 * h, 256), at(i, 384)]
-    act_copies = direct(act_view)
-
-    to_sibling(qkv_copies, qkv_own, qkv_cols)
-    arrive(table_copies)
-    table_own.wait()
+
+    arrive(g_near + g_far)
+    g_own.wait()
+    wo_load.wait()
+
+    def head_grads(n):
+        p = dot(cg[mine, :], wo[:, at(n, 256)]).astype(bf16)
+        hs[2 * n, :, 384:512] = p[:, :128]
+        hs[2 * n + 1, :, 384:512] = p[:, 128:]
+
+    loop(2, head_grads)
+    up_copies, up_own = to_heads(up_cols)
+    g_copies = direct(cg_view)
+    arrive(qkv_pair)
 
     def score_rows(i):
         part = at(i, 256)
         scores = contract_cols(heads[part, 0:128], heads[:, 128:256]) * scale
-        start = tables[part, 128:256][:, 127:128]
         query = (i * 256 + lax.broadcasted_iota(jnp.int32, (256, 1), 0)).astype(f32)
         key = lax.broadcasted_iota(jnp.int32, (256, 1024), 1).astype(f32)
-        return scores, (key <= query) & (key >= start)
+        return scores, (key <= query) & (key >= starts[part, 0:1])
 
     def forward(i):
         part = at(i, 256)
@@ -692,33 +742,10 @@
     for i in (0, 1):
         att[pl.ds(256 * i, 256), at(m, 128)] = attf[pl.ds(512 * i + 256 * c, 256), :].astype(bf16)
     att_copies = direct(att_view)
-
-    arrive(g_copies)
-    g_own.wait()
-    wo_load.wait()
-
-    def head_grads(n):
-        p = dot(cg[...], wo[:, at(n, 256)]).astype(bf16)
-        hs[2 * n, :, 384:512] = p[:, :128]
-        hs[2 * n + 1, :, 384:512] = p[:, 128:]
-
-    loop(2, head_grads)
-    up_copies, up_own = to_heads(up_cols)
-    cs_copies, cs_own = slices(cg, cs)
-    wd_load.wait()
-
-    def hidden(n):
-        cols = at(n, 256)
-        low = (dot(cg[...], wd[:, cols]) * gd[:, cols]).astype(bf16)
-        hid[mine, cols] = low
-        usum[6:7, cols] = jnp.sum(low.astype(f32), axis=0, keepdims=True)
-        usum[4:5, cols] = jnp.sum(cg[:, cols].astype(f32), axis=0, keepdims=True)
-
-    loop(8, hidden)
-
-    to_sibling(up_copies, up_own, up_cols)
+    up_pair = to_sibling(up_copies, up_own, up_cols)
     dk_acc[...] = jnp.zeros_like(dk_acc)
     dv_acc[...] = jnp.zeros_like(dv_acc)
+    arrive(up_pair)
 
     def backward(i):
         part = at(i, 256)
@@ -732,24 +759,58 @@
 
         @pl.when(i % 2 == c)
         def _():
+            here = at(i // 2, 256)
             back = dot(grads, heads[:, 128:256]) * scale
-            pack[at(i // 2, 256), at(3 * m, 128)] = turned(back, tables[part, :], -1.0).astype(bf16)
+            pack[here, at(3 * m, 128)] = turned(back, cosr[here, :], -sinr[here, :]).astype(bf16)
 
     loop(4, backward)
     for i in (0, 1):
-        part = pl.ds(512 * i + 256 * c, 256)
-        key_back = turned(dk_acc[part, :] * scale, tables[part, :], -1.0)
-        pack[pl.ds(256 * i, 256), at(3 * m + 1, 128)] = key_back.astype(bf16)
-        pack[pl.ds(256 * i, 256), at(3 * m + 2, 128)] = dv_acc[part, :].astype(bf16)
+        part, here = pl.ds(512 * i + 256 * c, 256), pl.ds(256 * i, 256)
+        key_back = turned(dk_acc[part, :] * scale, cosr[here, :], -sinr[here, :])
+        pack[here, at(3 * m + 1, 128)] = key_back.astype(bf16)
+        pack[here, at(3 * m + 2, 128)] = dv_acc[part, :].astype(bf16)
     pack_copies = direct(pack_view)
+    g_relays = relay(g_copies, cg_half)
     att_relays = relay(att_copies, att_half)
-    act_relays = relay(act_copies, act_half)
-    hid_copies = direct(hid_view)
+    arrive(x_relays + x_rest)
+    norm(flip4(m, 2), False)
+    norm(flip4(m, 3), False)
+    feed(1 - x)
+    pack_relays = relay(pack_copies, pack_half)
+    wd_load.wait()
 
     def feed_out(n):
         acco[n] = contract_cols(act[mine, :], wd[at(n, 256), :])
 
     loop(8, feed_out)
+    arrive(att_relays)
+
+    def finish_out(n):
+        ob[n % 4, n // 4] = (acco[n] + contract_cols(att[mine, :], wo[at(n, 256), :])).astype(bf16)
+
+    loop(8, finish_out)
+
+    def scatter(src, dst):
+        copies = [send(src.at[flip4(t, k)], dst.at[t], grid_peer(k)) for k in (1, 3, 2)]
+        return copies, move(src.at[t], dst.at[t])
+
+    def across(copies, kept, src, which):
+        arrive(copies)
+        kept.wait()
+        sums = [sum(src[i, half].astype(f32) for i in range(4)) for half in (0, 1)]
+        keep = jnp.where(b == 0, sums[0], sums[1])
+        swap_b[which] = jnp.where(b == 0, sums[1], sums[0]).astype(bf16)
+        return keep, send(swap_b.at[which], back_b.at[which], grid_peer(4))
+
+    out_copies, out_own = scatter(ob, ro)
+    arrive(g_relays)
+
+    def hidden(n):
+        cols = at(n, 256)
+        low = (dot(cg[...], wd[:, cols]) * gd[:, cols].astype(f32)).astype(bf16)
+        hid[:, cols] = low
+
+    loop(8, hidden)
 
     def norm_grad(n, values, weight, which):
         cols = at(n, 256)
@@ -759,65 +820,51 @@
         return ng * rows2[which, 0:1, cols]
 
     def feed_grad(n):
+        cols = at(n, 256)
         accg[n] = norm_grad(n, hid[mine, :], wu, 1)
+        usum[6:7, cols] = jnp.sum(hid[mine, cols].astype(f32), axis=0, keepdims=True)
+        usum[4:5, cols] = jnp.sum(cg[mine, cols].astype(f32), axis=0, keepdims=True)
 
     loop(8, feed_grad)
-    arrive(att_relays)
-
-    def finish_out(n):
-        ob[n] = (acco[n] + contract_cols(att[mine, :], wo[at(n, 256), :])).astype(bf16)
-
-    loop(8, finish_out)
-
-    def scatter(src, dst):
-        copies = [send(src.at[4 * grid_peer(k)[1] + grid_peer(k)[2]], dst.at[j], grid_peer(k))
-                  for k in range(1, 8)]
-        return copies, move(src.at[j], dst.at[j])
-
-    out_copies, out_own = scatter(ob, ro)
-    arrive(xs_copies + cs_copies)
-    for copy in xs_own + cs_own:
-        copy.wait()
+    arrive(pack_relays)
+
+    def attention_grad(n):
+        accg[n] += norm_grad(n, pack[mine, :], wp, 0)
+
+    loop(8, attention_grad)
+    usum[5:6, 0:1536] = jnp.sum(pack[mine, :].astype(f32), axis=0, keepdims=True)
+    pair_copy = send(usum, pair, sibling())
+    zero = jnp.zeros((128, 1), f32)
+
+    def means(n, carry):
+        g = accg[n]
+        return (carry[0] + jnp.sum(g, axis=-1, keepdims=True),
+                carry[1] + jnp.sum(g * xh[:, at(n, 256)], axis=-1, keepdims=True))
+
+    mean, slope = lax.fori_loop(0, 8, means, (zero, zero))
+    mean, slope = mean * (1.0 / 2048), slope * (1.0 / 2048)
+
+    def finish_grad(n):
+        gb[n % 4, n // 4] = (inv_s[mine, 0:1] * (accg[n] - mean - xh[:, at(n, 256)] * slope)).astype(bf16)
+
+    loop(8, finish_grad)
+    grad_copies, grad_own = scatter(gb, rg)
 
     def transpose_slices(i):
         part = at(i, 128)
         for half in (0, 1):
             cols = pl.ds(256 * half, 256)
-            block = at(4 * x + 2 * half + b, 256)
-            hat = xs[part, cols].astype(f32)
+            features = at(4 * x + 2 * half + b, 256)
+            hat = (xg[part, features].astype(f32) - mean_s[part, 0:1]) * inv_s[part, 0:1]
             for which, dst in ((0, n0t), (1, n1t)):
-                low = hat * rows2[which, 0:1, block] + rows2[which, 1:2, block]
+                low = hat * rows2[which, 0:1, features] + rows2[which, 1:2, features]
                 dst[cols, part] = low.T.astype(bf16)
-            ct[cols, part] = cs[part, cols].astype(f32).T.astype(bf16)
+            ct[cols, part] = cg[part, features].astype(f32).T.astype(bf16)
 
     loop(4, transpose_slices)
-
-    pack_relays = relay(pack_copies, pack_half)
-    arrive(pack_relays)
-
-    def attention_grad(n):
-        accg[n] += norm_grad(n, pack[mine, :], wp, 0)
-
-    loop(8, attention_grad)
-    usum[5:6, 0:1536] = jnp.sum(pack[mine, :].astype(f32), axis=0, keepdims=True)
-    pair_copy = send(usum, pair, sibling())
-
-    zero = jnp.zeros((128, 1), f32)
-
-    def means(n, carry):
-        g = accg[n]
-        return (carry[0] + jnp.sum(g, axis=-1, keepdims=True),
-                carry[1] + jnp.sum(g * xh[:, at(n, 256)], axis=-1, keepdims=True))
-
-    mean, slope = lax.fori_loop(0, 8, means, (zero, zero))
-    mean, slope = mean * (1.0 / 2048), slope * (1.0 / 2048)
-
-    def finish_grad(n):
-        gb[n] = (inv[:, 0:1] * (accg[n] - mean - xh[:, at(n, 256)] * slope)).astype(bf16)
-
-    loop(8, finish_grad)
-    grad_copies, grad_own = scatter(gb, rg)
-
+    arrive([pair_copy])
+    pair[...] += usum[...]
+    near_copies = [send(pair, near.at[k - 1], plane_peer(k)) for k in (1, 2, 3)]
     writes = []
 
     def matrix(lhs, rhs, count, out, base):
@@ -843,43 +890,29 @@
         done = []
         for i in range(count):
             swap(i).wait_recv()
-            own[i] += recv[base + i].astype(f32)
-            done.append(move(own.at[i], out.at[:, pl.ds(512 * i, 512)]))
+            low_own[i] = (own[i] + recv[base + i].astype(f32)).astype(bf16)
+            done.append(move(low_own.at[i], out.at[:, pl.ds(512 * i, 512)]))
             sent.append(swap(i))
         writes.append(done)
 
-    arrive(act_relays)
     matrix(ct, act, 4, down_o, 0)
-    hid_relays = relay(hid_copies, hid_half)
-    matrix(ct, att, 1, output_o, 4)
-    arrive([pair_copy])
-    pair[...] += usum[...]
-    near_copies = [send(pair, near.at[k - 1], plane_peer(k)) for k in (1, 2, 3)]
-    matrix(n0t, pack, 3, project_o, 5)
     arrive(near_copies)
     sums_o[t] = pair[...] + near[0] + near[1] + near[2]
     sum_copies = [send(sums_o.at[t], sums_o.at[t], grid_peer(k)) for k in (1, 2, 3)]
-    arrive(out_copies)
-    out_own.wait()
+    out_keep, out_swap = across(out_copies, out_own, ro, 0)
+    matrix(n1t, hid, 4, up_o, 4)
+    matrix(ct, att, 1, output_o, 8)
+    matrix(n0t, pack, 3, project_o, 9)
     columns = at(j, 256)
     bias = rows2[0, 2:3, columns] + rows2[1, 2:3, columns]
-    for h in (0, 1):
-        part = pl.ds(128 * h, 128)
-        total = bias + tok[part, :].astype(f32)
-        for i in range(4):
-            total = total + ro[4 * h + i].astype(f32)
-        layer_o[part, :] = total.astype(bf16)
-    arrive(grad_copies)
-    grad_own.wait()
-    for h in (0, 1):
-        part = pl.ds(128 * h, 128)
-        total = cot[part, :].astype(f32)
-        for i in range(4):
-            total = total + rg[4 * h + i].astype(f32)
-        grad_o[part, :] = total
-    arrive(hid_relays)
-    matrix(n1t, hid, 4, up_o, 8)
-    arrive(sum_copies)
+    here, there = at(b, 128), at(1 - b, 128)
+    layer_o[here, :] = (bias + tok[here, :].astype(f32) + out_keep).astype(bf16)
+    arrive([out_swap])
+    layer_o[there, :] = (bias + tok[there, :].astype(f32) + back_b[0].astype(f32)).astype(bf16)
+    grad_keep, grad_swap = across(grad_copies, grad_own, rg, 1)
+    grad_o[here, :] = cot[here, :].astype(f32) + grad_keep
+    arrive(sum_copies + [grad_swap])
+    grad_o[there, :] = cot[there, :].astype(f32) + back_b[1].astype(f32)
     for part in writes[-1]:
         part.wait()
     for copy in sent:
@@ -887,51 +920,76 @@
     assert used["sem"] <= 100 and used["local"] <= 40, used
 
 
+def emit_kernel(layer, grad, project, output, up, down, sums, layer_o, grad_o, project_o, output_o,
+                up_o, down_o, offs_o, hidden_o, gain_o, center_o, residual_o):
+    project_o[...] = project[...].astype(f32)
+    output_o[...] = output[...].astype(f32)
+    up_o[...] = up[...].astype(f32)
+    down_o[...] = down[...].astype(f32)
+
+    @pl.when(pl.program_id(0) == 0)
+    def _():
+        layer_o[...] = layer[...]
+        grad_o[...] = grad[...]
+        gain_o[...] = sums[0, 0:2] + sums[1, 0:2] + sums[2, 0:2] + sums[3, 0:2]
+        center_o[...] = sums[0, 2:4] + sums[1, 2:4] + sums[2, 2:4] + sums[3, 2:4]
+        residual_o[...] = jnp.broadcast_to(sums[0, 4:5], (2, 2048))
+        for i in range(4):
+            offs_o[pl.ds(1536 * i, 1536)] = sums[i, 5, 0:1536]
+            hidden_o[pl.ds(2048 * i, 2048)] = sums[i, 6]
+
+
 def fast_device(tokens, cotangent, documents, positions, project_weight, offsets, output_weight,
                 up_weight, hidden_bias, down_weight, norm_gain, norm_bias, residual_bias):
-    s = lax.axis_index("seq")
-    cosine, sines = rope_tables(positions)
-    token_index = s * 256 + jnp.arange(256, dtype=jnp.int32)
-    start = (token_index - positions).astype(f32)
-    table = jnp.concatenate([
-        cosine, cosine, jnp.ones((256, HEAD_DIM - ROT), f32),
-        -sines, sines, jnp.broadcast_to(start[:, None], (256, HEAD_DIM - ROT))], axis=1)
-    rows = jnp.concatenate([norm_gain, norm_bias, residual_bias, jnp.zeros((5, 2048), f32)], axis=0)
+    half = ROT // 2
+    frequency = rope_base ** (-(2.0 * jnp.arange(half, dtype=f32)) / ROT)
+    waves = jnp.broadcast_to(jnp.concatenate([frequency, frequency])[:, None], (ROT, 256))
     vmem, anywhere = pl.BlockSpec(memory_space=pltpu.VMEM), pl.BlockSpec(memory_space=pl.ANY)
     shape = jax.ShapeDtypeStruct
     low = lambda *size: pltpu.VMEM(size, bf16)
     full = lambda *size: pltpu.VMEM(size, f32)
-    layer_out, input_grad, project_grad, output_grad, up_grad, down_grad, sums = pl.pallas_call(
+    widths = (1536, 512, 2048, 2048)
+    results = pl.pallas_call(
         layer_kernel,
-        out_shape=[
-            shape((256, 256), bf16), shape((256, 256), f32), shape((256, 1536), f32),
-            shape((256, 512), f32), shape((256, 2048), f32), shape((256, 2048), f32),
-            shape((4, 8, 2048), f32)],
-        in_specs=[vmem] * 6 + [anywhere] * 4,
+        out_shape=[shape((256, 256), bf16), shape((256, 256), f32)]
+        + [shape((256, width), bf16) for width in widths] + [shape((4, 8, 2048), f32)],
+        in_specs=[vmem] * 9 + [anywhere] * 4,
         out_specs=[vmem] * 2 + [anywhere] * 4 + [vmem],
         scratch_shapes=[
             low(2048, 1536), low(2048, 512), low(2048, 2048), low(2048, 2048),
-            low(128, 2048), low(128, 2048), full(1024, 256), full(2, 8, 2048),
-            full(128, 2048), full(128, 128), low(128, 2048), low(128, 2048), low(128, 2048),
-            full(128, 2048), low(512, 2048), low(512, 2048), low(4, 128, 512), low(1024, 512),
-            low(512, 512), low(512, 1536), full(1024, 128), full(1024, 128), full(1024, 128),
-            full(1024, 128), low(8, 128, 256), low(8, 128, 256), low(8, 128, 256),
-            low(8, 128, 256), full(8, 128, 256), full(8, 128, 256), low(512, 512), low(512, 512),
-            low(512, 512), low(512, 512), low(512, 512), full(4, 256, 512), low(12, 256, 512),
+            low(512, 2048), low(512, 2048), full(4, 8, 256), full(1024, 128), full(512, 128),
+            full(512, 128), full(2, 8, 2048), full(128, 2048), full(512, 128), full(512, 128),
+            low(128, 2048), low(256, 2048), GD(512, 2048), low(512, 2048), low(512, 2048),
+            low(4, 128, 512), low(1024, 512), low(512, 512), low(512, 1536), full(1024, 128),
+            full(1024, 128), full(1024, 128), full(1024, 128), low(4, 2, 128, 256),
+            low(4, 2, 128, 256), low(4, 2, 128, 256), low(4, 2, 128, 256), low(2, 128, 256),
+            low(2, 128, 256), full(8, 128, 256), full(8, 128, 256), low(512, 512), low(512, 512),
+            low(512, 512), full(4, 256, 512), low(4, 256, 512), low(12, 256, 512),
             low(12, 256, 512), full(8, 2048), full(8, 2048), full(3, 8, 2048),
             pltpu.SemaphoreType.DMA((2, 100)), pltpu.SemaphoreType.DMA((40,))],
         compiler_params=pltpu.CompilerParams(
             collective_id=0, has_side_effects=True, vmem_limit_bytes=LIMIT),
-    )(tokens, cotangent, table, rows, offsets[None], hidden_bias[None], project_weight,
-      output_weight, up_weight, down_weight)
-    across = jnp.sum(sums[:, :4], axis=0)
-    return (
-        layer_out, input_grad, project_grad, output_grad, up_grad, down_grad,
-        sums[:, 5, :1536].reshape(6144), sums[:, 6].reshape(8192),
-        across[:2], across[2:], jnp.broadcast_to(sums[0, 4], (2, 2048)))
-
-
-LIMIT = 62 << 20
+    )(tokens, cotangent, positions[None], waves, norm_gain, norm_bias, residual_bias,
+      offsets[None], hidden_bias[None], project_weight, output_weight, up_weight, down_weight)
+    steps = 4
+    whole = lambda *size: pl.BlockSpec(size, lambda i: (0,) * len(size))
+    band = lambda width: pl.BlockSpec((256 // steps, width), lambda i: (i, 0))
+    layer_out, input_grad, *rest = pl.pallas_call(
+        emit_kernel,
+        grid=(steps,),
+        out_shape=[shape((256, 256), bf16), shape((256, 256), f32)]
+        + [shape((256, width), f32) for width in widths]
+        + [shape((6144,), f32), shape((8192,), f32)] + [shape((2, 2048), f32)] * 3,
+        in_specs=[whole(256, 256)] * 2 + [band(width) for width in widths] + [whole(4, 8, 2048)],
+        out_specs=[whole(256, 256)] * 2 + [band(width) for width in widths]
+        + [whole(6144), whole(8192)] + [whole(2, 2048)] * 3,
+        compiler_params=pltpu.CompilerParams(vmem_limit_bytes=32 << 20),
+    )(*results)
+    return (layer_out, input_grad, *rest)
+
+
+LIMIT = 63 << 20
+GD = lambda *size: pltpu.VMEM(size, bf16)
 
 
 def solution(mesh):

time: 157 us -> 121 us (0.77)
  Pallas kernels: 134 us -> 111 us
  local copies, waits for them, and re-layouts: 18.1 us -> 9.31 us
  other arithmetic: 3.78 us -> 0.09 us
    pallas_call x1, Pallas kernels: 134 us -> 107 us  [fast_device(): pl.pallas_call(layer_kernel, out_shape=[shape((256, 256), bf16), shape((2...]
    slice x4 -> x0, local copies, waits for them, and re-layouts: 4.62 us -> none  [the longest x1 1.59 us: fast_device(): sums[:, 6].reshape(8192)]
    unnamed x12 -> x14, local copies, waits for them, and re-layouts: 10.5 us -> 7.33 us
    pallas_call x0 -> x1, Pallas kernels: none -> 3.16 us  [fast_device(): pl.pallas_call(emit_kernel, grid=(steps,), out_shape=[shape((256, 256), b...]
where the time goes in v1:
time: 121 us
  Pallas kernels  111 us (92%)
  local copies, waits for them, and re-layouts  9.31 us (8%)
    pallas_call x1, Pallas kernels, fast_device(): pl.pallas_call(layer_kernel, out_shape=[shape((256, 256), bf16), shape((2...  107 us
    unnamed x14, local copies, waits for them, and re-layouts  7.33 us
    pallas_call x1, Pallas kernels, fast_device(): pl.pallas_call(emit_kernel, grid=(steps,), out_shape=[shape((256, 256), b...  3.16 us

profile of v1, /device:TPU:0, one launch (start us, length us, event | category | flops | bytes accessed | tf_op | source)
XLA Modules:
  0.0 120.7 jit_solution(17346387115263471168)
XLA Ops:
  0.7 0.1 pad_maximum_fusion
  0.7 1.3 %broadcast_in_dim.17.offs = f32[1,1536]{1,0:T(1,128)} reshape(f32[1536]{0:T(1024)} %param.17) | data formatting | bytes 12288 | tf_op jit(solution)/shard_map/broadcast_in_dim | solution.py:973
  2.0 0.7 broadcast_in_dim.16.waves
  2.7 107.5 %shard_map.203 = (bf16[256,256]{1,0:T(8,128)(2,1)}, f32[256,256]{1,0:T(8,128)}, bf16[256,1536]{1,0:T(8,128)(2,1)}, bf16[256,512]{1,0:T(8,128)(2,1)}, bf16[256,20...) custom-call(bf16[256,256]{1,0:T(8,128)(2,1)} %tok.1, bf16[256,256]{1,0:T(8,128)(2,1)} %cot.1, ...), custom_call_target="tpu_custom_call" | custom-call | tf_op jit(solution)/shard_map/pallas_call | solution.py:952
  110.2 0.0 copy-start
  110.2 1.2 %copy-done = bf16[256,2048]{1,0:T(8,128)(2,1)S(1)} copy-done((bf16[256,2048]{1,0:T(8,128)(2,1)S(1)}, bf16[256,2048]{1,0:T(8,128)(2,1)}, u32[]{:S(2)}) %copy-start) | copy-done | bytes 1048600
  111.4 0.0 copy-start.1
  111.4 1.2 %copy-done.1 = bf16[256,2048]{1,0:T(8,128)(2,1)S(1)} copy-done((bf16[256,2048]{1,0:T(8,128)(2,1)S(1)}, bf16[256,2048]{1,0:T(8,128)(2,1)}, u32[]{:S(2)}) %copy-start.1) | copy-done | bytes 1048600
  112.7 0.0 copy-start.2
  112.7 1.1 copy-done.2
  113.8 0.0 copy-start.3
  113.8 0.9 copy-done.3
  114.8 0.0 copy-start.4
  114.8 0.9 copy-done.4
  115.7 0.0 copy-start.5
  115.7 0.9 copy-done.5
  116.7 0.0 copy-start.6
  116.7 0.9 copy-done.6
  117.6 3.2 %shard_map.204 = (bf16[256,256]{1,0:T(8,128)(2,1)}, f32[256,256]{1,0:T(8,128)}, f32[256,1536]{1,0:T(8,128)}, f32[256,512]{1,0:T(8,128)}, f32[256,2048]{1,0:T(8,1...) custom-call(bf16[256,256]{1,0:T(8,128)(2,1)S(1)} %copy-done.6, ...), custom_call_target="tpu_custom_call" | custom-call | tf_op jit(solution)/shard_map/pallas_call | solution.py:977
  (1 shorter events, 0.0 us)
Async XLA Ops:
  110.2 1.2 %copy-start = (bf16[256,2048]{1,0:T(8,128)(2,1)S(1)}, bf16[256,2048]{1,0:T(8,128)(2,1)}, u32[]{:S(2)}) copy-start(bf16[256,2048]{1,0:T(8,128)(2,1)} %get-tuple-element.22.up) | copy-start | bytes 3145732
  111.4 1.2 %copy-start.1 = (bf16[256,2048]{1,0:T(8,128)(2,1)S(1)}, bf16[256,2048]{1,0:T(8,128)(2,1)}, u32[]{:S(2)}) copy-start(bf16[256,2048]{1,0:T(8,128)(2,1)} %get-tuple-element.23.down) | copy-start | bytes 3145732
  112.7 1.1 copy-start.2
  113.8 0.9 copy-start.3
  114.8 0.9 copy-start.4
  115.7 0.9 copy-start.5
  116.7 0.9 copy-start.6

commit v2 on v1

--- a/solution.py
+++ b/solution.py
@@ -519,11 +519,11 @@
 
 
 def layer_kernel(
-    tok, cot, places, waves, gain, shift, residual, offs, hbias, wp_h, wo_h, wu_h, wd_h,
+    tok, cot, places_h, gain_h, shift_h, residual_h, offs_h, hbias_h, wp_h, wo_h, wu_h, wd_h,
     layer_o, grad_o, project_o, output_o, up_o, down_o, sums_o,
-    wp, wo, wu, wd, xg, cg, posr, starts, cosr, sinr, rows2, xh, mean_s, inv_s, n0, n1, gd, act, hid,
-    hs, heads, att, pack, attf, lse, dk_acc, dv_acc, ob, ro, gb, rg, swap_b, back_b, acco, accg,
-    n0t, n1t, ct, own, low_own, other, recv, usum, pair, near, sems, local,
+    wp, wo, wu, wd, tok_v, cot_v, places, gain, shift, residual, offs, hbias, xg, cg, posr, starts, cosr, sinr, rows2, xh, mean_s, inv_s, n0, n1, gd, act, hid,
+    hs, heads, att, pack, attf, lse, dk_acc, dv_acc, ob, ro, gb, rg, swap_b, back_b, accg,
+    n0t, n1t, ct, other, recv, usum, pair, near, sems, local,
 ):
     s, b, t, x, c = place()
     m, j = 2 * x + b, 4 * b + t
@@ -531,16 +531,27 @@
     scale = HEAD_DIM ** -0.5
     mine = at(m, 128)
     used = {"sem": 0, "local": 0}
-    sent = []
-
-    def send(src, dst, device):
+    sent, inner_sent = [], []
+    inner = (t == 1) | (t == 2)
+
+    def describe(src, dst, device, there=None):
         index = used["sem"]
         used["sem"] += 1
-        copy = pltpu.make_async_remote_copy(
-            src_ref=src, dst_ref=dst, send_sem=sems.at[0, index], recv_sem=sems.at[1, index],
+        return pltpu.make_async_remote_copy(
+            src_ref=src, dst_ref=dst, send_sem=sems.at[0, index],
+            recv_sem=sems.at[1, index if there is None else there],
             device_id=device, device_id_type=MESH)
+
+    def send(src, dst, device):
+        copy = describe(src, dst, device)
         copy.start()
         sent.append(copy)
+        return copy
+
+    def send_inner(src, dst, device, there=None):
+        copy = describe(src, dst, device, there)
+        pl.when(inner)(copy.start)
+        inner_sent.append(copy)
         return copy
 
     def move(src, dst):
@@ -574,59 +585,92 @@
     def block(k):
         return at(4 * flip(b, k // 4) + flip4(t, k % 4), 256)
 
-    usum[...] = jnp.zeros_like(usum)
-    wp_load, wo_load = move(wp_h, wp), move(wo_h, wo)
-    wu_load, wd_load = move(wu_h, wu), move(wd_h, wd)
+    def gather(src, dst):
+        over = send(src.at[at(1 - b, 128)], dst.at[at(flip4(m, 1), 128), at(j, 256)], grid_peer(4))
+        half = src.at[at(b, 128)]
+        near = to_tensor(half, dst.at[mine, at(j, 256)])
+        return {"over": over, "near": near, "own": move(half, dst.at[mine, at(j, 256)]), "dst": dst,
+                "plane": {}}
+
+    def to_tensor(src, dst):
+        last = used["sem"]
+        third = send_inner(src, dst, grid_peer(3))
+        return {2: send(src, dst, grid_peer(2)), 1: send(src, dst, grid_peer(1)), 3: third, "last": last}
+
+    def on_plane(state, k):
+        part = state["dst"].at[mine, block(k)]
+        state["plane"][k] = [send(part, part, plane_peer(i)) for i in (2, 1)]
+
+    def gather_over(state):
+        state["own"].wait()
+        state["over"].wait_recv()
+        part = state["dst"].at[mine, block(4)]
+        state["far"] = to_tensor(part, part)
+
+    def gather_step(state, k):
+        for which, first in (("near", 0), ("far", 4)):
+            state[which][k].wait_recv()
+            if k == 2:
+                part = state["dst"].at[mine, block(first + 2)]
+                send_inner(part, part, grid_peer(1), state[which]["last"])
+
+    def both_on_plane(state, k):
+        on_plane(state, k)
+        on_plane(state, k + 4)
+
+    def plane_relay(state, k, here=False):
+        dst, plane = state["dst"], state["plane"]
+        plane[k][0].wait_recv()
+        part = dst.at[at(flip4(m, 2), 128), block(k)]
+        first = send(part, part, plane_peer(1))
+        if not here:
+            plane[k + 4][1].wait_recv()
+        part = dst.at[at(flip4(m, 1), 128), block(k)]
+        return [first, send(part, part, plane_peer(2)), plane[k + 4][0]]
+
+    meet([grid_peer(k) for k in (1, 2, 3, 4)] + [plane_peer(2), plane_peer(3)]
+         + [(flip4(s, k), b, t) for k in (1, 3)])
+    x_state = gather(tok, xg)
+    small = [move(src, dst) for src, dst in (
+        (places_h, places), (gain_h, gain), (shift_h, shift), (residual_h, residual),
+        (offs_h, offs), (hbias_h, hbias))]
+    wp_load, wu_load = move(wp_h, wp), move(wu_h, wu)
+    wo_load, wd_load = move(wo_h, wo), move(wd_h, wd)
+    late = [move(tok, tok_v), move(cot, cot_v)]
+    for copy in small:
+        copy.wait()
     rows2[b] = jnp.zeros((8, 2048), f32)
     rows2[b, 0:1, :] = gain[...]
     rows2[b, 1:2, :] = shift[...]
     rows2[b, 2:3, :] = residual[...]
-    posr[s] = jnp.broadcast_to(places[...].astype(f32), (8, 256))
-    meet([grid_peer(k) for k in (1, 2, 3, 4)] + [plane_peer(2), plane_peer(3)]
-         + [(flip4(s, k), b, t) for k in (1, 3)])
-
-    def gather_first(src, dst):
-        over = send(src.at[at(1 - b, 128)], dst.at[at(flip4(m, 1), 128), at(j, 256)], grid_peer(4))
-        half = src.at[at(b, 128)]
-        copies = [send(half, dst.at[mine, at(j, 256)], grid_peer(k)) for k in (1, 3, 2)]
-        return over, copies, move(half, dst.at[mine, at(j, 256)])
-
-    def gather_second(over, dst):
-        over.wait_recv()
-        part = dst.at[mine, block(4)]
-        return [send(part, part, grid_peer(k)) for k in (1, 3, 2)]
-
-    x_over, x_near, x_own = gather_first(tok, xg)
+    posr[s] = jnp.broadcast_to(places[...].astype(f32)[None, :], (8, 256))
     row_copy = send(rows2.at[b], rows2.at[b], grid_peer(4))
     place_copies = [send(posr.at[s], posr.at[s], (flip4(s, k), b, t)) for k in (1, 2, 3)]
-    spread = {}
-
-    def on_plane(k):
-        part = xg.at[mine, block(k)]
-        spread[k] = [send(part, part, plane_peer(i)) for i in (2, 1)]
-
-    x_own.wait()
-    on_plane(0)
-    x_far = gather_second(x_over, xg)
-    on_plane(4)
+    gather_over(x_state)
+    both_on_plane(x_state, 0)
+    usum[...] = jnp.zeros_like(usum)
+    dk_acc[...] = jnp.zeros_like(dk_acc)
+    dv_acc[...] = jnp.zeros_like(dv_acc)
     arrive(place_copies)
     for i in range(4):
         row = jnp.broadcast_to(posr[i, 0:1, :], (128, 256))
         index = (256 * i + lax.broadcasted_iota(jnp.int32, (256, 128), 0)).astype(f32)
         starts[pl.ds(256 * i, 256), :] = index - row.T
+    line = lax.broadcasted_iota(jnp.int32, (ROT, 256), 0)
+    waves = jnp.zeros((ROT, 256), f32)
+    for i in range(ROT // 2):
+        waves = jnp.where(line % (ROT // 2) == i, rope_base ** (-2.0 * i / ROT), waves)
     for i in (0, 1):
-        angle = posr[2 * i + c, 0:1, :] * waves[...]
+        angle = posr[2 * i + c, 0:1, :] * waves
         part = pl.ds(256 * i, 256)
-        sign = jnp.where(lax.broadcasted_iota(jnp.int32, (ROT, 256), 0) < ROT // 2, -1.0, 1.0)
+        sign = jnp.where(line < ROT // 2, -1.0, 1.0)
         rest = jnp.zeros((HEAD_DIM - ROT, 256), f32)
         cosr[part, :] = jnp.concatenate([jnp.cos(angle), rest + 1.0], axis=0).T
         sinr[part, :] = jnp.concatenate([jnp.sin(angle) * sign, rest], axis=0).T
-    for i, k in enumerate((1, 3, 2)):
-        x_near[i].wait_recv()
-        on_plane(k)
-        x_far[i].wait_recv()
-        on_plane(k + 4)
-    g_over, g_near, g_own = gather_first(cot, cg)
+    for k in (1, 2, 3):
+        gather_step(x_state, k)
+        both_on_plane(x_state, k)
+    g_state = gather(cot, cg)
     arrive([row_copy])
 
     def norm(which, whole):
@@ -648,12 +692,15 @@
         loop(8, rows)
 
     norm(m, True)
-    g_far = gather_second(g_over, cg)
+    gather_over(g_state)
+    x_relays = []
+    for k in (0, 1, 2):
+        x_relays += plane_relay(x_state, k)
     wp_load.wait()
     turn = pl.ds(pl.multiple_of(256 * x + 128 * b, 128), 128)
 
     def project(h):
-        p = dot(n0[...], wp[:, at(h, 384)]) + offs[:, at(h, 384)]
+        p = dot(n0[...], wp[:, at(h, 384)]) + offs[at(h, 384)][None, :]
         hs[h, :, 0:128] = turned(p[:, 0:128], cosr[turn, :], sinr[turn, :]).astype(bf16)
         hs[h, :, 128:256] = turned(p[:, 128:256], cosr[turn, :], sinr[turn, :]).astype(bf16)
         hs[h, :, 256:384] = p[:, 256:384].astype(bf16)
@@ -673,125 +720,108 @@
 
     qkv_cols, up_cols = pl.ds(0, 384), pl.ds(384, 128)
     qkv_copies, qkv_own = to_heads(qkv_cols)
-    x_relays, x_rest = [], []
-    for k in range(4):
-        spread[k][0].wait_recv()
-        part = xg.at[at(flip4(m, 2), 128), block(k)]
-        x_relays.append(send(part, part, plane_peer(1)))
-        spread[k + 4][1].wait_recv()
-        part = xg.at[at(flip4(m, 1), 128), block(k)]
-        x_relays.append(send(part, part, plane_peer(2)))
-        x_rest.append(spread[k + 4][0])
-    arrive([spread[k][1] for k in range(4)])
+    x_relays += plane_relay(x_state, 3)
+    gather_step(g_state, 1)
+    arrive([x_state["plane"][k][1] for k in range(4)])
     norm(flip4(m, 1), False)
     wu_load.wait()
 
-    def feed(pair_index):
+    def feed(pair_index, first, count):
         rows = at(pair_index, 256)
 
         def tile(n):
-            cols = at(n, 256)
-            u = dot(n1[...], wu[:, cols]) + hbias[:, cols]
+            cols = at(first + n, 512)
+            u = dot(n1[...], wu[:, cols]) + hbias[cols][None, :]
             phi = 0.5 + 0.5 * lax.erf(u * 0.7071067811865476)
             act[rows, cols] = (u * phi).astype(bf16)
             gd[rows, cols] = (phi + u * (0.3989422804014327 * jnp.exp(-0.5 * u * u))).astype(gd.dtype)
 
-        loop(8, tile)
-
-    feed(x)
+        loop(count, tile)
+
+    feed(x, 0, 2)
+    gather_step(g_state, 2)
+    feed(x, 2, 2)
     qkv_pair = to_sibling(qkv_copies, qkv_own, qkv_cols)
-    cg_view = lambda i: cg.at[at(i, 128)]
-    cg_half = lambda i, h: cg.at[pl.ds(pl.multiple_of(128 * i + 64 * h, 64), 64)]
     att_view = lambda i: att.at[:, at(i, 128)]
     att_half = lambda i, h: att.at[pl.ds(256 * h, 256), at(i, 128)]
     pack_view = lambda i: pack.at[:, at(i, 384)]
     pack_half = lambda i, h: pack.at[pl.ds(256 * h, 256), at(i, 384)]
 
-    arrive(g_near + g_far)
-    g_own.wait()
+    def score_rows(i):
+        width = 256 * (i + 1)
+        part = pl.ds(256 * i, 256)
+        scores = contract_cols(heads[part, 0:128], heads[0:width, 128:256]) * scale
+        query = (256 * i + lax.broadcasted_iota(jnp.int32, (256, 1), 0)).astype(f32)
+        key = lax.broadcasted_iota(jnp.int32, (256, width), 1).astype(f32)
+        visible = (key <= query) & (key >= starts[part, 0:1])
+        return part, width, jnp.where(visible, scores, masked_score), visible
+
+    gather_step(g_state, 3)
     wo_load.wait()
 
-    def head_grads(n):
-        p = dot(cg[mine, :], wo[:, at(n, 256)]).astype(bf16)
-        hs[2 * n, :, 384:512] = p[:, :128]
-        hs[2 * n + 1, :, 384:512] = p[:, 128:]
-
-    loop(2, head_grads)
+    head_low = dot(cg[mine, :], wo[...]).astype(bf16)
+    for h in range(4):
+        hs[h, :, 384:512] = head_low[:, 128 * h : 128 * (h + 1)]
     up_copies, up_own = to_heads(up_cols)
-    g_copies = direct(cg_view)
+    for k in range(4):
+        both_on_plane(g_state, k)
     arrive(qkv_pair)
-
-    def score_rows(i):
-        part = at(i, 256)
-        scores = contract_cols(heads[part, 0:128], heads[:, 128:256]) * scale
-        query = (i * 256 + lax.broadcasted_iota(jnp.int32, (256, 1), 0)).astype(f32)
-        key = lax.broadcasted_iota(jnp.int32, (256, 1024), 1).astype(f32)
-        return scores, (key <= query) & (key >= starts[part, 0:1])
-
-    def forward(i):
-        part = at(i, 256)
-        scores, visible = score_rows(i)
-        masked = jnp.where(visible, scores, masked_score)
+    for i in range(4):
+        part, width, masked, visible = score_rows(i)
         top = jnp.max(masked, axis=-1, keepdims=True)
         weights = jnp.where(visible, jnp.exp(masked - top), 0.0)
         total = jnp.sum(weights, axis=-1, keepdims=True)
-        attf[part, :] = dot(weights.astype(bf16), heads[:, 256:384]) / total
+        attf[part, :] = dot(weights.astype(bf16), heads[0:width, 256:384]) / total
         lse[part, :] = jnp.broadcast_to(top + jnp.log(total), (256, 128))
 
-    loop(4, forward)
     for i in (0, 1):
         att[pl.ds(256 * i, 256), at(m, 128)] = attf[pl.ds(512 * i + 256 * c, 256), :].astype(bf16)
     att_copies = direct(att_view)
+    arrive(x_relays)
+    norm(flip4(m, 2), False)
     up_pair = to_sibling(up_copies, up_own, up_cols)
-    dk_acc[...] = jnp.zeros_like(dk_acc)
-    dv_acc[...] = jnp.zeros_like(dv_acc)
+    norm(flip4(m, 3), False)
+    wd_load.wait()
+
+    def feed_out(n):
+        accg[:, at(n, 1024)] = contract_cols(act[mine, :], wd[at(n, 1024), :])
+
+    loop(2, feed_out)
+    att_relays = relay(att_copies, att_half)
     arrive(up_pair)
 
-    def backward(i):
-        part = at(i, 256)
-        scores, visible = score_rows(i)
-        probs = jnp.where(visible, jnp.exp(jnp.where(visible, scores, masked_score) - lse[part, 0:1]), 0.0)
+    for i in range(4):
+        part, width, masked, visible = score_rows(i)
+        probs = jnp.where(visible, jnp.exp(masked - lse[part, 0:1]), 0.0)
         up = heads[part, 384:512]
         delta = jnp.sum(up.astype(f32) * attf[part, :], axis=-1, keepdims=True)
-        grads = (probs * (contract_cols(up, heads[:, 256:384]) - delta)).astype(bf16)
-        dv_acc[...] += contract_rows(probs.astype(bf16), up)
-        dk_acc[...] += contract_rows(grads, heads[part, 0:128])
+        grads = (probs * (contract_cols(up, heads[0:width, 256:384]) - delta)).astype(bf16)
+        dv_acc[0:width, :] += contract_rows(probs.astype(bf16), up)
+        dk_acc[0:width, :] += contract_rows(grads, heads[part, 0:128])
 
         @pl.when(i % 2 == c)
         def _():
-            here = at(i // 2, 256)
-            back = dot(grads, heads[:, 128:256]) * scale
+            here = pl.ds(256 * (i // 2), 256)
+            back = dot(grads, heads[0:width, 128:256]) * scale
             pack[here, at(3 * m, 128)] = turned(back, cosr[here, :], -sinr[here, :]).astype(bf16)
 
-    loop(4, backward)
     for i in (0, 1):
         part, here = pl.ds(512 * i + 256 * c, 256), pl.ds(256 * i, 256)
         key_back = turned(dk_acc[part, :] * scale, cosr[here, :], -sinr[here, :])
         pack[here, at(3 * m + 1, 128)] = key_back.astype(bf16)
         pack[here, at(3 * m + 2, 128)] = dv_acc[part, :].astype(bf16)
     pack_copies = direct(pack_view)
-    g_relays = relay(g_copies, cg_half)
-    att_relays = relay(att_copies, att_half)
-    arrive(x_relays + x_rest)
-    norm(flip4(m, 2), False)
-    norm(flip4(m, 3), False)
-    feed(1 - x)
-    pack_relays = relay(pack_copies, pack_half)
-    wd_load.wait()
-
-    def feed_out(n):
-        acco[n] = contract_cols(act[mine, :], wd[at(n, 256), :])
-
-    loop(8, feed_out)
     arrive(att_relays)
 
     def finish_out(n):
-        ob[n % 4, n // 4] = (acco[n] + contract_cols(att[mine, :], wo[at(n, 256), :])).astype(bf16)
-
-    loop(8, finish_out)
+        total = accg[:, at(n, 1024)] + contract_cols(att[mine, :], wo[at(n, 1024), :])
+        for i in range(4):
+            ob[i, n] = total[:, 256 * i : 256 * (i + 1)].astype(bf16)
+
+    loop(2, finish_out)
 
     def scatter(src, dst):
-        copies = [send(src.at[flip4(t, k)], dst.at[t], grid_peer(k)) for k in (1, 3, 2)]
+        copies = [send(src.at[flip4(t, k)], dst.at[t], grid_peer(k)) for k in (3, 2, 1)]
         return copies, move(src.at[t], dst.at[t])
 
     def across(copies, kept, src, which):
@@ -803,41 +833,50 @@
         return keep, send(swap_b.at[which], back_b.at[which], grid_peer(4))
 
     out_copies, out_own = scatter(ob, ro)
-    arrive(g_relays)
-
-    def hidden(n):
-        cols = at(n, 256)
-        low = (dot(cg[...], wd[:, cols]) * gd[:, cols].astype(f32)).astype(bf16)
-        hid[:, cols] = low
-
-    loop(8, hidden)
+
+    def hidden(pair_index):
+        rows = at(pair_index, 256)
+
+        def tile(n):
+            cols = at(n, 512)
+            hid[rows, cols] = (dot(cg[rows, :], wd[:, cols]) * gd[rows, cols].astype(f32)).astype(bf16)
+
+        loop(4, tile)
+
+    arrive([g_state["plane"][k][1] for k in range(8)])
+    hidden(x)
+    feed(1 - x, 0, 4)
+    pack_relays = relay(pack_copies, pack_half)
+    g_relays = []
+    for k in range(4):
+        g_relays += plane_relay(g_state, k, True)
 
     def norm_grad(n, values, weight, which):
-        cols = at(n, 256)
+        cols = at(n, 512)
         ng = contract_cols(values, weight[cols, :])
         usum[which : which + 1, cols] = jnp.sum(ng * xh[:, cols], axis=0, keepdims=True)
         usum[which + 2 : which + 3, cols] = jnp.sum(ng, axis=0, keepdims=True)
         return ng * rows2[which, 0:1, cols]
 
     def feed_grad(n):
-        cols = at(n, 256)
-        accg[n] = norm_grad(n, hid[mine, :], wu, 1)
+        cols = at(n, 512)
+        accg[:, cols] = norm_grad(n, hid[mine, :], wu, 1)
         usum[6:7, cols] = jnp.sum(hid[mine, cols].astype(f32), axis=0, keepdims=True)
         usum[4:5, cols] = jnp.sum(cg[mine, cols].astype(f32), axis=0, keepdims=True)
 
-    loop(8, feed_grad)
+    loop(4, feed_grad)
     arrive(pack_relays)
 
     def attention_grad(n):
-        accg[n] += norm_grad(n, pack[mine, :], wp, 0)
-
-    loop(8, attention_grad)
+        accg[:, at(n, 512)] += norm_grad(n, pack[mine, :], wp, 0)
+
+    loop(4, attention_grad)
     usum[5:6, 0:1536] = jnp.sum(pack[mine, :].astype(f32), axis=0, keepdims=True)
     pair_copy = send(usum, pair, sibling())
     zero = jnp.zeros((128, 1), f32)
 
     def means(n, carry):
-        g = accg[n]
+        g = accg[:, at(n, 256)]
         return (carry[0] + jnp.sum(g, axis=-1, keepdims=True),
                 carry[1] + jnp.sum(g * xh[:, at(n, 256)], axis=-1, keepdims=True))
 
@@ -845,10 +884,12 @@
     mean, slope = mean * (1.0 / 2048), slope * (1.0 / 2048)
 
     def finish_grad(n):
-        gb[n % 4, n // 4] = (inv_s[mine, 0:1] * (accg[n] - mean - xh[:, at(n, 256)] * slope)).astype(bf16)
+        gb[n % 4, n // 4] = (inv_s[mine, 0:1] * (accg[:, at(n, 256)] - mean - xh[:, at(n, 256)] * slope)).astype(bf16)
 
     loop(8, finish_grad)
     grad_copies, grad_own = scatter(gb, rg)
+    arrive(g_relays)
+    hidden(1 - x)
 
     def transpose_slices(i):
         part = at(i, 128)
@@ -868,9 +909,6 @@
     writes = []
 
     def matrix(lhs, rhs, count, out, base):
-        for copy in writes[-1:]:
-            for part in copy:
-                part.wait()
         first = used["sem"]
         used["sem"] += count
 
@@ -884,16 +922,18 @@
             right = rhs[:, at(i, 512)]
             other[base + i] = dot(lhs[at(1 - c, 256), :], right).astype(bf16)
             swap(i).start()
-            own[i] = dot(lhs[at(c, 256), :], right)
+            kept = dot(lhs[at(c, 256), :], right)
+            xh[:, at(i, 512)] = kept[:128]
+            accg[:, at(i, 512)] = kept[128:]
 
         loop(count, produce)
-        done = []
         for i in range(count):
             swap(i).wait_recv()
-            low_own[i] = (own[i] + recv[base + i].astype(f32)).astype(bf16)
-            done.append(move(low_own.at[i], out.at[:, pl.ds(512 * i, 512)]))
+            for part, kept in ((pl.ds(0, 128), xh), (pl.ds(128, 128), accg)):
+                total = kept[:, pl.ds(512 * i, 512)] + recv[base + i, part, :].astype(f32)
+                recv[base + i, part, :] = total.astype(bf16)
+            writes.append(move(recv.at[base + i], out.at[:, pl.ds(512 * i, 512)]))
             sent.append(swap(i))
-        writes.append(done)
 
     matrix(ct, act, 4, down_o, 0)
     arrive(near_copies)
@@ -903,21 +943,25 @@
     matrix(n1t, hid, 4, up_o, 4)
     matrix(ct, att, 1, output_o, 8)
     matrix(n0t, pack, 3, project_o, 9)
+    for copy in late:
+        copy.wait()
     columns = at(j, 256)
     bias = rows2[0, 2:3, columns] + rows2[1, 2:3, columns]
     here, there = at(b, 128), at(1 - b, 128)
-    layer_o[here, :] = (bias + tok[here, :].astype(f32) + out_keep).astype(bf16)
+    layer_o[here, :] = (bias + tok_v[here, :].astype(f32) + out_keep).astype(bf16)
     arrive([out_swap])
-    layer_o[there, :] = (bias + tok[there, :].astype(f32) + back_b[0].astype(f32)).astype(bf16)
+    layer_o[there, :] = (bias + tok_v[there, :].astype(f32) + back_b[0].astype(f32)).astype(bf16)
     grad_keep, grad_swap = across(grad_copies, grad_own, rg, 1)
-    grad_o[here, :] = cot[here, :].astype(f32) + grad_keep
+    grad_o[here, :] = cot_v[here, :].astype(f32) + grad_keep
     arrive(sum_copies + [grad_swap])
-    grad_o[there, :] = cot[there, :].astype(f32) + back_b[1].astype(f32)
-    for part in writes[-1]:
-        part.wait()
+    grad_o[there, :] = cot_v[there, :].astype(f32) + back_b[1].astype(f32)
+    for copy in writes:
+        copy.wait()
     for copy in sent:
         copy.wait_send()
-    assert used["sem"] <= 100 and used["local"] <= 40, used
+    for copy in inner_sent:
+        pl.when(inner)(copy.wait_send)
+    assert used["sem"] <= 150 and used["local"] <= 40, used
 
 
 def emit_kernel(layer, grad, project, output, up, down, sums, layer_o, grad_o, project_o, output_o,
@@ -941,9 +985,6 @@
 
 def fast_device(tokens, cotangent, documents, positions, project_weight, offsets, output_weight,
                 up_weight, hidden_bias, down_weight, norm_gain, norm_bias, residual_bias):
-    half = ROT // 2
-    frequency = rope_base ** (-(2.0 * jnp.arange(half, dtype=f32)) / ROT)
-    waves = jnp.broadcast_to(jnp.concatenate([frequency, frequency])[:, None], (ROT, 256))
     vmem, anywhere = pl.BlockSpec(memory_space=pltpu.VMEM), pl.BlockSpec(memory_space=pl.ANY)
     shape = jax.ShapeDtypeStruct
     low = lambda *size: pltpu.VMEM(size, bf16)
@@ -953,25 +994,27 @@
         layer_kernel,
         out_shape=[shape((256, 256), bf16), shape((256, 256), f32)]
         + [shape((256, width), bf16) for width in widths] + [shape((4, 8, 2048), f32)],
-        in_specs=[vmem] * 9 + [anywhere] * 4,
+        in_specs=[anywhere] * 12,
         out_specs=[vmem] * 2 + [anywhere] * 4 + [vmem],
         scratch_shapes=[
             low(2048, 1536), low(2048, 512), low(2048, 2048), low(2048, 2048),
+            low(256, 256), low(256, 256), pltpu.VMEM((256,), jnp.int32), full(1, 2048), full(1, 2048),
+            full(1, 2048), full(1536), full(2048),
             low(512, 2048), low(512, 2048), full(4, 8, 256), full(1024, 128), full(512, 128),
             full(512, 128), full(2, 8, 2048), full(128, 2048), full(512, 128), full(512, 128),
             low(128, 2048), low(256, 2048), GD(512, 2048), low(512, 2048), low(512, 2048),
             low(4, 128, 512), low(1024, 512), low(512, 512), low(512, 1536), full(1024, 128),
             full(1024, 128), full(1024, 128), full(1024, 128), low(4, 2, 128, 256),
             low(4, 2, 128, 256), low(4, 2, 128, 256), low(4, 2, 128, 256), low(2, 128, 256),
-            low(2, 128, 256), full(8, 128, 256), full(8, 128, 256), low(512, 512), low(512, 512),
-            low(512, 512), full(4, 256, 512), low(4, 256, 512), low(12, 256, 512),
+            low(2, 128, 256), full(128, 2048), low(512, 512), low(512, 512),
+            low(512, 512), low(12, 256, 512),
             low(12, 256, 512), full(8, 2048), full(8, 2048), full(3, 8, 2048),
-            pltpu.SemaphoreType.DMA((2, 100)), pltpu.SemaphoreType.DMA((40,))],
+            pltpu.SemaphoreType.DMA((2, 150)), pltpu.SemaphoreType.DMA((40,))],
         compiler_params=pltpu.CompilerParams(
             collective_id=0, has_side_effects=True, vmem_limit_bytes=LIMIT),
-    )(tokens, cotangent, positions[None], waves, norm_gain, norm_bias, residual_bias,
-      offsets[None], hidden_bias[None], project_weight, output_weight, up_weight, down_weight)
-    steps = 4
+    )(tokens, cotangent, positions, norm_gain, norm_bias, residual_bias,
+      offsets, hidden_bias, project_weight, output_weight, up_weight, down_weight)
+    steps = 2
     whole = lambda *size: pl.BlockSpec(size, lambda i: (0,) * len(size))
     band = lambda width: pl.BlockSpec((256 // steps, width), lambda i: (i, 0))
     layer_out, input_grad, *rest = pl.pallas_call(
@@ -983,7 +1026,7 @@
         in_specs=[whole(256, 256)] * 2 + [band(width) for width in widths] + [whole(4, 8, 2048)],
         out_specs=[whole(256, 256)] * 2 + [band(width) for width in widths]
         + [whole(6144), whole(8192)] + [whole(2, 2048)] * 3,
-        compiler_params=pltpu.CompilerParams(vmem_limit_bytes=32 << 20),
+        compiler_params=pltpu.CompilerParams(vmem_limit_bytes=LIMIT),
     )(*results)
     return (layer_out, input_grad, *rest)
 

time: 121 us -> 102 us (0.84)
  Pallas kernels: 111 us -> 101 us
  local copies, waits for them, and re-layouts: 9.31 us -> 0 us
    pallas_call x1, Pallas kernels: 107 us -> 96.7 us  [fast_device(): pl.pallas_call(layer_kernel, out_shape=[shape((256, 256), bf16), shape((2...]
    unnamed x14 -> x0, local copies, waits for them, and re-layouts: 7.33 us -> none
    broadcast_in_dim x2 -> x0, local copies, waits for them, and re-layouts: 1.98 us -> none  [the longest x1 1.3 us: fast_device(): offsets[None]]
    pallas_call x1, Pallas kernels: 3.16 us -> 4.73 us  [fast_device(): pl.pallas_call(emit_kernel, grid=(steps,), out_shape=[shape((256, 256), b...]
where the time goes in v2:
time: 102 us
  Pallas kernels  101 us (99%)
    pallas_call x1, Pallas kernels, fast_device(): pl.pallas_call(layer_kernel, out_shape=[shape((256, 256), bf16), shape((2...  96.7 us
    pallas_call x1, Pallas kernels, fast_device(): pl.pallas_call(emit_kernel, grid=(steps,), out_shape=[shape((256, 256), b...  4.73 us

profile of v2, /device:TPU:0, one launch (start us, length us, event | category | flops | bytes accessed | tf_op | source)
XLA Modules:
  0.0 102.2 jit_solution(7228566587143489795)
XLA Ops:
  0.6 96.7 %shard_map.203 = (bf16[256,256]{1,0:T(8,128)(2,1)}, f32[256,256]{1,0:T(8,128)}, bf16[256,1536]{1,0:T(8,128)(2,1)}, bf16[256,512]{1,0:T(8,128)(2,1)}, bf16[256,20...) custom-call(bf16[256,256]{1,0:T(8,128)(2,1)} %tok.1, bf16[256,256]{1,0:T(8,128)(2,1)} %cot.1, ...), custom_call_target="tpu_custom_call" | custom-call | tf_op jit(solution)/shard_map/pallas_call | solution.py:993
  97.4 4.7 %shard_map.204 = (bf16[256,256]{1,0:T(8,128)(2,1)}, f32[256,256]{1,0:T(8,128)}, f32[256,1536]{1,0:T(8,128)}, f32[256,512]{1,0:T(8,128)}, f32[256,2048]{1,0:T(8,1...) custom-call(bf16[256,256]{1,0:T(8,128)(2,1)} %get-tuple-element.18.l, ...), custom_call_target="tpu_custom_call" | custom-call | tf_op jit(solution)/shard_map/pallas_call | solution.py:1020

commit v3 on v2

--- a/solution.py
+++ b/solution.py
@@ -520,10 +520,10 @@
 
 def layer_kernel(
     tok, cot, places_h, gain_h, shift_h, residual_h, offs_h, hbias_h, wp_h, wo_h, wu_h, wd_h,
-    layer_o, grad_o, project_o, output_o, up_o, down_o, sums_o,
+    layer_o, grad_o, kept_o, came_o, sums_o,
     wp, wo, wu, wd, tok_v, cot_v, places, gain, shift, residual, offs, hbias, xg, cg, posr, starts, cosr, sinr, rows2, xh, mean_s, inv_s, n0, n1, gd, act, hid,
     hs, heads, att, pack, attf, lse, dk_acc, dv_acc, ob, ro, gb, rg, swap_b, back_b, accg,
-    n0t, n1t, ct, other, recv, usum, pair, near, sems, local,
+    n0t, n1t, ct, other, kept, usum, pair, near, sems, local,
 ):
     s, b, t, x, c = place()
     m, j = 2 * x + b, 4 * b + t
@@ -586,11 +586,13 @@
         return at(4 * flip(b, k // 4) + flip4(t, k % 4), 256)
 
     def gather(src, dst):
+        half, place = src.at[at(b, 128)], dst.at[mine, at(j, 256)]
         over = send(src.at[at(1 - b, 128)], dst.at[at(flip4(m, 1), 128), at(j, 256)], grid_peer(4))
-        half = src.at[at(b, 128)]
-        near = to_tensor(half, dst.at[mine, at(j, 256)])
-        return {"over": over, "near": near, "own": move(half, dst.at[mine, at(j, 256)]), "dst": dst,
+        return {"over": over, "half": half, "place": place, "own": move(half, place), "dst": dst,
                 "plane": {}}
+
+    def gather_near(state):
+        state["near"] = to_tensor(state["half"], state["place"])
 
     def to_tensor(src, dst):
         last = used["sem"]
@@ -631,6 +633,8 @@
     meet([grid_peer(k) for k in (1, 2, 3, 4)] + [plane_peer(2), plane_peer(3)]
          + [(flip4(s, k), b, t) for k in (1, 3)])
     x_state = gather(tok, xg)
+    gather_near(x_state)
+    g_state = gather(cot, cg)
     small = [move(src, dst) for src, dst in (
         (places_h, places), (gain_h, gain), (shift_h, shift), (residual_h, residual),
         (offs_h, offs), (hbias_h, hbias))]
@@ -670,7 +674,9 @@
     for k in (1, 2, 3):
         gather_step(x_state, k)
         both_on_plane(x_state, k)
-    g_state = gather(cot, cg)
+        if k == 2:
+            gather_near(g_state)
+            gather_over(g_state)
     arrive([row_copy])
 
     def norm(which, whole):
@@ -692,7 +698,6 @@
         loop(8, rows)
 
     norm(m, True)
-    gather_over(g_state)
     x_relays = []
     for k in (0, 1, 2):
         x_relays += plane_relay(x_state, k)
@@ -740,7 +745,6 @@
 
     feed(x, 0, 2)
     gather_step(g_state, 2)
-    feed(x, 2, 2)
     qkv_pair = to_sibling(qkv_copies, qkv_own, qkv_cols)
     att_view = lambda i: att.at[:, at(i, 128)]
     att_half = lambda i, h: att.at[pl.ds(256 * h, 256), at(i, 128)]
@@ -756,15 +760,6 @@
         visible = (key <= query) & (key >= starts[part, 0:1])
         return part, width, jnp.where(visible, scores, masked_score), visible
 
-    gather_step(g_state, 3)
-    wo_load.wait()
-
-    head_low = dot(cg[mine, :], wo[...]).astype(bf16)
-    for h in range(4):
-        hs[h, :, 384:512] = head_low[:, 128 * h : 128 * (h + 1)]
-    up_copies, up_own = to_heads(up_cols)
-    for k in range(4):
-        both_on_plane(g_state, k)
     arrive(qkv_pair)
     for i in range(4):
         part, width, masked, visible = score_rows(i)
@@ -776,18 +771,18 @@
 
     for i in (0, 1):
         att[pl.ds(256 * i, 256), at(m, 128)] = attf[pl.ds(512 * i + 256 * c, 256), :].astype(bf16)
+    gather_step(g_state, 3)
+    wo_load.wait()
+
+    head_low = dot(cg[mine, :], wo[...]).astype(bf16)
+    for h in range(4):
+        hs[h, :, 384:512] = head_low[:, 128 * h : 128 * (h + 1)]
+    up_copies, up_own = to_heads(up_cols)
     att_copies = direct(att_view)
-    arrive(x_relays)
-    norm(flip4(m, 2), False)
+    both_on_plane(g_state, 0)
+    both_on_plane(g_state, 1)
+    feed(x, 2, 2)
     up_pair = to_sibling(up_copies, up_own, up_cols)
-    norm(flip4(m, 3), False)
-    wd_load.wait()
-
-    def feed_out(n):
-        accg[:, at(n, 1024)] = contract_cols(act[mine, :], wd[at(n, 1024), :])
-
-    loop(2, feed_out)
-    att_relays = relay(att_copies, att_half)
     arrive(up_pair)
 
     for i in range(4):
@@ -810,7 +805,19 @@
         key_back = turned(dk_acc[part, :] * scale, cosr[here, :], -sinr[here, :])
         pack[here, at(3 * m + 1, 128)] = key_back.astype(bf16)
         pack[here, at(3 * m + 2, 128)] = dv_acc[part, :].astype(bf16)
+    att_relays = relay(att_copies, att_half)
     pack_copies = direct(pack_view)
+    both_on_plane(g_state, 2)
+    both_on_plane(g_state, 3)
+    arrive(x_relays)
+    norm(flip4(m, 2), False)
+    norm(flip4(m, 3), False)
+    wd_load.wait()
+
+    def feed_out(n):
+        accg[:, at(n, 1024)] = contract_cols(act[mine, :], wd[at(n, 1024), :])
+
+    loop(2, feed_out)
     arrive(att_relays)
 
     def finish_out(n):
@@ -834,22 +841,14 @@
 
     out_copies, out_own = scatter(ob, ro)
 
-    def hidden(pair_index):
-        rows = at(pair_index, 256)
-
+    def hidden(rows):
         def tile(n):
             cols = at(n, 512)
             hid[rows, cols] = (dot(cg[rows, :], wd[:, cols]) * gd[rows, cols].astype(f32)).astype(bf16)
 
         loop(4, tile)
 
-    arrive([g_state["plane"][k][1] for k in range(8)])
-    hidden(x)
-    feed(1 - x, 0, 4)
-    pack_relays = relay(pack_copies, pack_half)
-    g_relays = []
-    for k in range(4):
-        g_relays += plane_relay(g_state, k, True)
+    hidden(mine)
 
     def norm_grad(n, values, weight, which):
         cols = at(n, 512)
@@ -865,6 +864,24 @@
         usum[4:5, cols] = jnp.sum(cg[mine, cols].astype(f32), axis=0, keepdims=True)
 
     loop(4, feed_grad)
+    pack_relays = relay(pack_copies, pack_half)
+    feed(1 - x, 0, 4)
+    arrive([g_state["plane"][k][1] for k in range(8)])
+    g_relays = []
+    for k in range(4):
+        g_relays += plane_relay(g_state, k, True)
+    def transpose_tokens(i):
+        part = at(i, 128)
+        for half in (0, 1):
+            cols = pl.ds(256 * half, 256)
+            features = at(4 * x + 2 * flip(c, half) + b, 256)
+            hat = (xg[part, features].astype(f32) - mean_s[part, 0:1]) * inv_s[part, 0:1]
+            for which, dst in ((0, n0t), (1, n1t)):
+                low = hat * rows2[which, 0:1, features] + rows2[which, 1:2, features]
+                dst[cols, part] = low.T.astype(bf16)
+
+    loop(4, transpose_tokens)
+    hidden(at(flip4(m, 1), 128))
     arrive(pack_relays)
 
     def attention_grad(n):
@@ -888,61 +905,55 @@
 
     loop(8, finish_grad)
     grad_copies, grad_own = scatter(gb, rg)
+    writes, swaps = [], []
+
+    def matrix(lhs, rhs, count, base):
+        first, here = used["sem"], used["local"]
+        used["sem"] += count
+        used["local"] += count
+
+        def swap(i):
+            return pltpu.make_async_remote_copy(
+                src_ref=other.at[base + i], dst_ref=came_o.at[base + i],
+                send_sem=sems.at[0, first + i], recv_sem=sems.at[1, first + i],
+                device_id=sibling(), device_id_type=MESH)
+
+        def keep(i):
+            return pltpu.make_async_copy(kept.at[base + i], kept_o.at[base + i], local.at[here + i])
+
+        def produce(i):
+            both = dot(lhs[...], rhs[:, at(i, 512)]).astype(bf16)
+            other[base + i] = both[256:]
+            swap(i).start()
+            kept[base + i] = both[:256]
+            keep(i).start()
+
+        loop(count, produce)
+        for i in range(count):
+            writes.append(keep(i))
+            swaps.append(swap(i))
+
+    matrix(n0t, pack, 3, 9)
     arrive(g_relays)
-    hidden(1 - x)
-
-    def transpose_slices(i):
+    hidden(at(1 - x, 256))
+
+    def transpose_grads(i):
         part = at(i, 128)
         for half in (0, 1):
-            cols = pl.ds(256 * half, 256)
-            features = at(4 * x + 2 * half + b, 256)
-            hat = (xg[part, features].astype(f32) - mean_s[part, 0:1]) * inv_s[part, 0:1]
-            for which, dst in ((0, n0t), (1, n1t)):
-                low = hat * rows2[which, 0:1, features] + rows2[which, 1:2, features]
-                dst[cols, part] = low.T.astype(bf16)
-            ct[cols, part] = cg[part, features].astype(f32).T.astype(bf16)
-
-    loop(4, transpose_slices)
+            features = at(4 * x + 2 * flip(c, half) + b, 256)
+            ct[pl.ds(256 * half, 256), part] = cg[part, features].astype(f32).T.astype(bf16)
+
+    loop(4, transpose_grads)
     arrive([pair_copy])
     pair[...] += usum[...]
     near_copies = [send(pair, near.at[k - 1], plane_peer(k)) for k in (1, 2, 3)]
-    writes = []
-
-    def matrix(lhs, rhs, count, out, base):
-        first = used["sem"]
-        used["sem"] += count
-
-        def swap(i):
-            return pltpu.make_async_remote_copy(
-                src_ref=other.at[base + i], dst_ref=recv.at[base + i],
-                send_sem=sems.at[0, first + i], recv_sem=sems.at[1, first + i],
-                device_id=sibling(), device_id_type=MESH)
-
-        def produce(i):
-            right = rhs[:, at(i, 512)]
-            other[base + i] = dot(lhs[at(1 - c, 256), :], right).astype(bf16)
-            swap(i).start()
-            kept = dot(lhs[at(c, 256), :], right)
-            xh[:, at(i, 512)] = kept[:128]
-            accg[:, at(i, 512)] = kept[128:]
-
-        loop(count, produce)
-        for i in range(count):
-            swap(i).wait_recv()
-            for part, kept in ((pl.ds(0, 128), xh), (pl.ds(128, 128), accg)):
-                total = kept[:, pl.ds(512 * i, 512)] + recv[base + i, part, :].astype(f32)
-                recv[base + i, part, :] = total.astype(bf16)
-            writes.append(move(recv.at[base + i], out.at[:, pl.ds(512 * i, 512)]))
-            sent.append(swap(i))
-
-    matrix(ct, act, 4, down_o, 0)
+    matrix(ct, act, 4, 0)
     arrive(near_copies)
     sums_o[t] = pair[...] + near[0] + near[1] + near[2]
     sum_copies = [send(sums_o.at[t], sums_o.at[t], grid_peer(k)) for k in (1, 2, 3)]
     out_keep, out_swap = across(out_copies, out_own, ro, 0)
-    matrix(n1t, hid, 4, up_o, 4)
-    matrix(ct, att, 1, output_o, 8)
-    matrix(n0t, pack, 3, project_o, 9)
+    matrix(n1t, hid, 4, 4)
+    matrix(ct, att, 1, 8)
     for copy in late:
         copy.wait()
     columns = at(j, 256)
@@ -955,7 +966,7 @@
     grad_o[here, :] = cot_v[here, :].astype(f32) + grad_keep
     arrive(sum_copies + [grad_swap])
     grad_o[there, :] = cot_v[there, :].astype(f32) + back_b[1].astype(f32)
-    for copy in writes:
+    for copy in writes + swaps:
         copy.wait()
     for copy in sent:
         copy.wait_send()
@@ -964,12 +975,11 @@
     assert used["sem"] <= 150 and used["local"] <= 40, used
 
 
-def emit_kernel(layer, grad, project, output, up, down, sums, layer_o, grad_o, project_o, output_o,
+def emit_kernel(layer, grad, kept, came, sums, layer_o, grad_o, project_o, output_o,
                 up_o, down_o, offs_o, hidden_o, gain_o, center_o, residual_o):
-    project_o[...] = project[...].astype(f32)
-    output_o[...] = output[...].astype(f32)
-    up_o[...] = up[...].astype(f32)
-    down_o[...] = down[...].astype(f32)
+    for out, base, count in ((down_o, 0, 4), (up_o, 4, 4), (output_o, 8, 1), (project_o, 9, 3)):
+        for i in range(count):
+            out[:, pl.ds(512 * i, 512)] = kept[base + i].astype(f32) + came[base + i].astype(f32)
 
     @pl.when(pl.program_id(0) == 0)
     def _():
@@ -993,9 +1003,9 @@
     results = pl.pallas_call(
         layer_kernel,
         out_shape=[shape((256, 256), bf16), shape((256, 256), f32)]
-        + [shape((256, width), bf16) for width in widths] + [shape((4, 8, 2048), f32)],
+        + [shape((12, 256, 512), bf16)] * 2 + [shape((4, 8, 2048), f32)],
         in_specs=[anywhere] * 12,
-        out_specs=[vmem] * 2 + [anywhere] * 4 + [vmem],
+        out_specs=[vmem] * 2 + [anywhere] * 2 + [vmem],
         scratch_shapes=[
             low(2048, 1536), low(2048, 512), low(2048, 2048), low(2048, 2048),
             low(256, 256), low(256, 256), pltpu.VMEM((256,), jnp.int32), full(1, 2048), full(1, 2048),
@@ -1023,7 +1033,8 @@
         out_shape=[shape((256, 256), bf16), shape((256, 256), f32)]
         + [shape((256, width), f32) for width in widths]
         + [shape((6144,), f32), shape((8192,), f32)] + [shape((2, 2048), f32)] * 3,
-        in_specs=[whole(256, 256)] * 2 + [band(width) for width in widths] + [whole(4, 8, 2048)],
+        in_specs=[whole(256, 256)] * 2
+        + [pl.BlockSpec((12, 256 // steps, 512), lambda i: (0, i, 0))] * 2 + [whole(4, 8, 2048)],
         out_specs=[whole(256, 256)] * 2 + [band(width) for width in widths]
         + [whole(6144), whole(8192)] + [whole(2, 2048)] * 3,
         compiler_params=pltpu.CompilerParams(vmem_limit_bytes=LIMIT),

time: 102 us -> 98.9 us (0.970)
  Pallas kernels: 101 us -> 98 us
    pallas_call x1, Pallas kernels: 96.7 us -> 92.8 us  [fast_device(): pl.pallas_call(layer_kernel, out_shape=[shape((256, 256), bf16), shape((2...]
where the time goes in v3:
time: 98.9 us; the launch traced here: 98.8 us
  Pallas kernels  98 us (99%)
    pallas_call x1, Pallas kernels, fast_device(): pl.pallas_call(layer_kernel, out_shape=[shape((256, 256), bf16), shape((2...  92.8 us
    pallas_call x1, Pallas kernels, fast_device(): pl.pallas_call(emit_kernel, grid=(steps,), out_shape=[shape((256, 256), b...  5.23 us

profile of v3, /device:TPU:0, one launch (start us, length us, event | category | flops | bytes accessed | tf_op | source)
XLA Modules:
  0.0 98.8 jit_solution(16718735275471713939)
XLA Ops:
  0.6 92.8 %shard_map.203 = (bf16[256,256]{1,0:T(8,128)(2,1)}, f32[256,256]{1,0:T(8,128)}, bf16[12,256,512]{2,1,0:T(8,128)(2,1)}, bf16[12,256,512]{2,1,0:T(8,128)(2,1)}, f32[4,8,2048]{2,1,0:T(8,128)}) custom-call(bf16[256,256]{1,0:T(8,128)(2,1)} %tok.1, bf16[256,256]{1,0:T(8,128)(2,1)} %cot.1, s32[256]{0:T(256)} %places_h.1, f32[1,2048]{1,0:T(1,128)} %gain_h.1, ...), custom_call_target="tpu_custom_call" | custom-call | tf_op jit(solution)/shard_map/pallas_call | solution.py:1003
  93.4 5.2 %shard_map.204 = (bf16[256,256]{1,0:T(8,128)(2,1)}, f32[256,256]{1,0:T(8,128)}, f32[256,1536]{1,0:T(8,128)}, f32[256,512]{1,0:T(8,128)}, f32[256,2048]{1,0:T(8,1...) custom-call(bf16[256,256]{1,0:T(8,128)(2,1)} %get-tuple-element.16.l, ...), custom_call_target="tpu_custom_call" | custom-call | tf_op jit(solution)/shard_map/pallas_call | solution.py:1030

commit v4 on v3

--- a/solution.py
+++ b/solution.py
@@ -681,21 +681,21 @@
 
     def norm(which, whole):
         def rows(i):
-            part = pl.ds(pl.multiple_of(which * 128 + 16 * i, 16), 16)
+            part = pl.ds(pl.multiple_of(which * 128 + 32 * i, 32), 32)
             v = xg[part, :].astype(f32)
             mean = jnp.mean(v, axis=-1, keepdims=True)
             centered = v - mean
             inverse = lax.rsqrt(jnp.mean(centered * centered, axis=-1, keepdims=True) + norm_eps)
             hat = centered * inverse
-            mean_s[part, :] = jnp.broadcast_to(mean, (16, 128))
-            inv_s[part, :] = jnp.broadcast_to(inverse, (16, 128))
-            n1_part = pl.ds(pl.multiple_of((which % 2) * 128 + 16 * i, 16), 16)
+            mean_s[part, :] = jnp.broadcast_to(mean, (32, 128))
+            inv_s[part, :] = jnp.broadcast_to(inverse, (32, 128))
+            n1_part = pl.ds(pl.multiple_of((which % 2) * 128 + 32 * i, 32), 32)
             n1[n1_part, :] = (hat * rows2[1, 0:1, :] + rows2[1, 1:2, :]).astype(bf16)
             if whole:
-                xh[at(i, 16), :] = hat
-                n0[at(i, 16), :] = (hat * rows2[0, 0:1, :] + rows2[0, 1:2, :]).astype(bf16)
-
-        loop(8, rows)
+                xh[at(i, 32), :] = hat
+                n0[at(i, 32), :] = (hat * rows2[0, 0:1, :] + rows2[0, 1:2, :]).astype(bf16)
+
+        loop(4, rows)
 
     norm(m, True)
     x_relays = []
@@ -729,6 +729,7 @@
     gather_step(g_state, 1)
     arrive([x_state["plane"][k][1] for k in range(4)])
     norm(flip4(m, 1), False)
+    gather_step(g_state, 2)
     wu_load.wait()
 
     def feed(pair_index, first, count):
@@ -744,7 +745,6 @@
         loop(count, tile)
 
     feed(x, 0, 2)
-    gather_step(g_state, 2)
     qkv_pair = to_sibling(qkv_copies, qkv_own, qkv_cols)
     att_view = lambda i: att.at[:, at(i, 128)]
     att_half = lambda i, h: att.at[pl.ds(256 * h, 256), at(i, 128)]
@@ -760,6 +760,13 @@
         visible = (key <= query) & (key >= starts[part, 0:1])
         return part, width, jnp.where(visible, scores, masked_score), visible
 
+    gather_step(g_state, 3)
+    wo_load.wait()
+
+    head_low = dot(cg[mine, :], wo[...]).astype(bf16)
+    for h in range(4):
+        hs[h, :, 384:512] = head_low[:, 128 * h : 128 * (h + 1)]
+    up_copies, up_own = to_heads(up_cols)
     arrive(qkv_pair)
     for i in range(4):
         part, width, masked, visible = score_rows(i)
@@ -771,17 +778,9 @@
 
     for i in (0, 1):
         att[pl.ds(256 * i, 256), at(m, 128)] = attf[pl.ds(512 * i + 256 * c, 256), :].astype(bf16)
-    gather_step(g_state, 3)
-    wo_load.wait()
-
-    head_low = dot(cg[mine, :], wo[...]).astype(bf16)
-    for h in range(4):
-        hs[h, :, 384:512] = head_low[:, 128 * h : 128 * (h + 1)]
-    up_copies, up_own = to_heads(up_cols)
     att_copies = direct(att_view)
     both_on_plane(g_state, 0)
     both_on_plane(g_state, 1)
-    feed(x, 2, 2)
     up_pair = to_sibling(up_copies, up_own, up_cols)
     arrive(up_pair)
 
@@ -809,6 +808,7 @@
     pack_copies = direct(pack_view)
     both_on_plane(g_state, 2)
     both_on_plane(g_state, 3)
+    feed(x, 2, 2)
     arrive(x_relays)
     norm(flip4(m, 2), False)
     norm(flip4(m, 3), False)
@@ -851,19 +851,19 @@
     hidden(mine)
 
     def norm_grad(n, values, weight, which):
-        cols = at(n, 512)
+        cols = at(n, 1024)
         ng = contract_cols(values, weight[cols, :])
         usum[which : which + 1, cols] = jnp.sum(ng * xh[:, cols], axis=0, keepdims=True)
         usum[which + 2 : which + 3, cols] = jnp.sum(ng, axis=0, keepdims=True)
         return ng * rows2[which, 0:1, cols]
 
     def feed_grad(n):
-        cols = at(n, 512)
+        cols = at(n, 1024)
         accg[:, cols] = norm_grad(n, hid[mine, :], wu, 1)
         usum[6:7, cols] = jnp.sum(hid[mine, cols].astype(f32), axis=0, keepdims=True)
         usum[4:5, cols] = jnp.sum(cg[mine, cols].astype(f32), axis=0, keepdims=True)
 
-    loop(4, feed_grad)
+    loop(2, feed_grad)
     pack_relays = relay(pack_copies, pack_half)
     feed(1 - x, 0, 4)
     arrive([g_state["plane"][k][1] for k in range(8)])
@@ -885,9 +885,9 @@
     arrive(pack_relays)
 
     def attention_grad(n):
-        accg[:, at(n, 512)] += norm_grad(n, pack[mine, :], wp, 0)
-
-    loop(4, attention_grad)
+        accg[:, at(n, 1024)] += norm_grad(n, pack[mine, :], wp, 0)
+
+    loop(2, attention_grad)
     usum[5:6, 0:1536] = jnp.sum(pack[mine, :].astype(f32), axis=0, keepdims=True)
     pair_copy = send(usum, pair, sibling())
     zero = jnp.zeros((128, 1), f32)
@@ -953,6 +953,7 @@
     sum_copies = [send(sums_o.at[t], sums_o.at[t], grid_peer(k)) for k in (1, 2, 3)]
     out_keep, out_swap = across(out_copies, out_own, ro, 0)
     matrix(n1t, hid, 4, 4)
+    grad_keep, grad_swap = across(grad_copies, grad_own, rg, 1)
     matrix(ct, att, 1, 8)
     for copy in late:
         copy.wait()
@@ -962,7 +963,6 @@
     layer_o[here, :] = (bias + tok_v[here, :].astype(f32) + out_keep).astype(bf16)
     arrive([out_swap])
     layer_o[there, :] = (bias + tok_v[there, :].astype(f32) + back_b[0].astype(f32)).astype(bf16)
-    grad_keep, grad_swap = across(grad_copies, grad_own, rg, 1)
     grad_o[here, :] = cot_v[here, :].astype(f32) + grad_keep
     arrive(sum_copies + [grad_swap])
     grad_o[there, :] = cot_v[there, :].astype(f32) + back_b[1].astype(f32)

time: 98.9 us -> 97.7 us (0.988)
  Pallas kernels: 98 us -> 96.8 us
    pallas_call x1, Pallas kernels: 92.8 us -> 91.6 us  [fast_device(): pl.pallas_call(layer_kernel, out_shape=[shape((256, 256), bf16), shape((2...]
where the time goes in v4:
time: 97.7 us; the launch traced here: 97.6 us
  Pallas kernels  96.8 us (99%)
    pallas_call x1, Pallas kernels, fast_device(): pl.pallas_call(layer_kernel, out_shape=[shape((256, 256), bf16), shape((2...  91.6 us
    pallas_call x1, Pallas kernels, fast_device(): pl.pallas_call(emit_kernel, grid=(steps,), out_shape=[shape((256, 256), b...  5.23 us

profile of v4, /device:TPU:0, one launch (start us, length us, event | category | flops | bytes accessed | tf_op | source)
XLA Modules:
  0.0 97.6 jit_solution(9216228816217869067)
XLA Ops:
  0.6 91.6 %shard_map.203 = (bf16[256,256]{1,0:T(8,128)(2,1)}, f32[256,256]{1,0:T(8,128)}, bf16[12,256,512]{2,1,0:T(8,128)(2,1)}, bf16[12,256,512]{2,1,0:T(8,128)(2,1)}, f32[4,8,2048]{2,1,0:T(8,128)}) custom-call(bf16[256,256]{1,0:T(8,128)(2,1)} %tok.1, bf16[256,256]{1,0:T(8,128)(2,1)} %cot.1, s32[256]{0:T(256)} %places_h.1, f32[1,2048]{1,0:T(1,128)} %gain_h.1, ...), custom_call_target="tpu_custom_call" | custom-call | tf_op jit(solution)/shard_map/pallas_call | solution.py:1003
  92.2 5.2 %shard_map.204 = (bf16[256,256]{1,0:T(8,128)(2,1)}, f32[256,256]{1,0:T(8,128)}, f32[256,1536]{1,0:T(8,128)}, f32[256,512]{1,0:T(8,128)}, f32[256,2048]{1,0:T(8,1...) custom-call(bf16[256,256]{1,0:T(8,128)(2,1)} %get-tuple-element.16.l, ...), custom_call_target="tpu_custom_call" | custom-call | tf_op jit(solution)/shard_map/pallas_call | solution.py:1030

commit v5 on v4

--- a/solution.py
+++ b/solution.py
@@ -597,7 +597,8 @@
     def to_tensor(src, dst):
         last = used["sem"]
         third = send_inner(src, dst, grid_peer(3))
-        return {2: send(src, dst, grid_peer(2)), 1: send(src, dst, grid_peer(1)), 3: third, "last": last}
+        near = send(src, dst, grid_peer(1))
+        return {2: send(src, dst, grid_peer(2)), 1: near, 3: third, "last": last}
 
     def on_plane(state, k):
         part = state["dst"].at[mine, block(k)]
@@ -704,13 +705,15 @@
     wp_load.wait()
     turn = pl.ds(pl.multiple_of(256 * x + 128 * b, 128), 128)
 
-    def project(h):
-        p = dot(n0[...], wp[:, at(h, 384)]) + offs[at(h, 384)][None, :]
-        hs[h, :, 0:128] = turned(p[:, 0:128], cosr[turn, :], sinr[turn, :]).astype(bf16)
-        hs[h, :, 128:256] = turned(p[:, 128:256], cosr[turn, :], sinr[turn, :]).astype(bf16)
-        hs[h, :, 256:384] = p[:, 256:384].astype(bf16)
-
-    loop(4, project)
+    def project(n):
+        both = dot(n0[...], wp[:, at(n, 768)]) + offs[at(n, 768)][None, :]
+        for i in (0, 1):
+            h, p = 2 * n + i, both[:, 384 * i : 384 * (i + 1)]
+            hs[h, :, 0:128] = turned(p[:, 0:128], cosr[turn, :], sinr[turn, :]).astype(bf16)
+            hs[h, :, 128:256] = turned(p[:, 128:256], cosr[turn, :], sinr[turn, :]).astype(bf16)
+            hs[h, :, 256:384] = p[:, 256:384].astype(bf16)
+
+    loop(2, project)
 
     def to_heads(cols):
         copies = [send(hs.at[flip4(m, k), :, cols], heads.at[at(slot, 128), cols], plane_peer(k))
@@ -841,14 +844,14 @@
 
     out_copies, out_own = scatter(ob, ro)
 
-    def hidden(rows):
+    def hidden(rows, width=512):
         def tile(n):
-            cols = at(n, 512)
+            cols = at(n, width)
             hid[rows, cols] = (dot(cg[rows, :], wd[:, cols]) * gd[rows, cols].astype(f32)).astype(bf16)
 
-        loop(4, tile)
-
-    hidden(mine)
+        loop(2048 // width, tile)
+
+    hidden(mine, 1024)
 
     def norm_grad(n, values, weight, which):
         cols = at(n, 1024)
@@ -866,10 +869,6 @@
     loop(2, feed_grad)
     pack_relays = relay(pack_copies, pack_half)
     feed(1 - x, 0, 4)
-    arrive([g_state["plane"][k][1] for k in range(8)])
-    g_relays = []
-    for k in range(4):
-        g_relays += plane_relay(g_state, k, True)
     def transpose_tokens(i):
         part = at(i, 128)
         for half in (0, 1):
@@ -881,7 +880,11 @@
                 dst[cols, part] = low.T.astype(bf16)
 
     loop(4, transpose_tokens)
-    hidden(at(flip4(m, 1), 128))
+    arrive([g_state["plane"][k][1] for k in range(8)])
+    g_relays = []
+    for k in range(4):
+        g_relays += plane_relay(g_state, k, True)
+    hidden(at(flip4(m, 1), 128), 1024)
     arrive(pack_relays)
 
     def attention_grad(n):

time: 97.7 us -> 97.6 us (level)
  no operation moved by 1% of the time
where the time goes in v5:
time: 97.6 us; the launch traced here: 97.4 us
  Pallas kernels  96.6 us (99%)
    pallas_call x1, Pallas kernels, fast_device(): pl.pallas_call(layer_kernel, out_shape=[shape((256, 256), bf16), shape((2...  91.4 us
    pallas_call x1, Pallas kernels, fast_device(): pl.pallas_call(emit_kernel, grid=(steps,), out_shape=[shape((256, 256), b...  5.23 us

profile of v5, /device:TPU:0, one launch (start us, length us, event | category | flops | bytes accessed | tf_op | source)
XLA Modules:
  0.0 97.4 jit_solution(12270780784285772211)
XLA Ops:
  0.6 91.4 %shard_map.203 = (bf16[256,256]{1,0:T(8,128)(2,1)}, f32[256,256]{1,0:T(8,128)}, bf16[12,256,512]{2,1,0:T(8,128)(2,1)}, bf16[12,256,512]{2,1,0:T(8,128)(2,1)}, f32[4,8,2048]{2,1,0:T(8,128)}) custom-call(bf16[256,256]{1,0:T(8,128)(2,1)} %tok.1, bf16[256,256]{1,0:T(8,128)(2,1)} %cot.1, s32[256]{0:T(256)} %places_h.1, f32[1,2048]{1,0:T(1,128)} %gain_h.1, ...), custom_call_target="tpu_custom_call" | custom-call | tf_op jit(solution)/shard_map/pallas_call | solution.py:1006
  92.0 5.2 %shard_map.204 = (bf16[256,256]{1,0:T(8,128)(2,1)}, f32[256,256]{1,0:T(8,128)}, f32[256,1536]{1,0:T(8,128)}, f32[256,512]{1,0:T(8,128)}, f32[256,2048]{1,0:T(8,1...) custom-call(bf16[256,256]{1,0:T(8,128)(2,1)} %get-tuple-element.16.l, ...), custom_call_target="tpu_custom_call" | custom-call | tf_op jit(solution)/shard_map/pallas_call | solution.py:1033

commit v6 on v4

--- a/solution.py
+++ b/solution.py
@@ -597,7 +597,8 @@
     def to_tensor(src, dst):
         last = used["sem"]
         third = send_inner(src, dst, grid_peer(3))
-        return {2: send(src, dst, grid_peer(2)), 1: send(src, dst, grid_peer(1)), 3: third, "last": last}
+        near = send(src, dst, grid_peer(1))
+        return {2: send(src, dst, grid_peer(2)), 1: near, 3: third, "last": last}
 
     def on_plane(state, k):
         part = state["dst"].at[mine, block(k)]

time: 97.7 us -> 97.6 us (level)
  no operation moved by 1% of the time
where the time goes in v6:
time: 97.6 us; the launch traced here: 97.4 us
  Pallas kernels  96.6 us (99%)
    pallas_call x1, Pallas kernels, fast_device(): pl.pallas_call(layer_kernel, out_shape=[shape((256, 256), bf16), shape((2...  91.4 us
    pallas_call x1, Pallas kernels, fast_device(): pl.pallas_call(emit_kernel, grid=(steps,), out_shape=[shape((256, 256), b...  5.23 us

profile of v6, /device:TPU:0, one launch (start us, length us, event | category | flops | bytes accessed | tf_op | source)
XLA Modules:
  0.0 97.4 jit_solution(1629724689331255607)
XLA Ops:
  0.6 91.4 %shard_map.203 = (bf16[256,256]{1,0:T(8,128)(2,1)}, f32[256,256]{1,0:T(8,128)}, bf16[12,256,512]{2,1,0:T(8,128)(2,1)}, bf16[12,256,512]{2,1,0:T(8,128)(2,1)}, f32[4,8,2048]{2,1,0:T(8,128)}) custom-call(bf16[256,256]{1,0:T(8,128)(2,1)} %tok.1, bf16[256,256]{1,0:T(8,128)(2,1)} %cot.1, s32[256]{0:T(256)} %places_h.1, f32[1,2048]{1,0:T(1,128)} %gain_h.1, ...), custom_call_target="tpu_custom_call" | custom-call | tf_op jit(solution)/shard_map/pallas_call | solution.py:1004
  92.0 5.2 %shard_map.204 = (bf16[256,256]{1,0:T(8,128)(2,1)}, f32[256,256]{1,0:T(8,128)}, f32[256,1536]{1,0:T(8,128)}, f32[256,512]{1,0:T(8,128)}, f32[256,2048]{1,0:T(8,1...) custom-call(bf16[256,256]{1,0:T(8,128)(2,1)} %get-tuple-element.16.l, ...), custom_call_target="tpu_custom_call" | custom-call | tf_op jit(solution)/shard_map/pallas_call | solution.py:1031
